TPU v7x, 256 devices: a whole 4x4x8 slice. The times are simulated.
256 devices in a mesh: seq: 64 (over y, z, core), ch: 4 (over x).
Axes of the slice: x: 4, y: 4, z: 8, core: 2. Of those that a mesh axis runs over, the one named last changes fastest.
Arguments:
- gated_input: bfloat16 [262144, 1024], P('seq', 'ch'), may hold values from -6 to 6
- out_gate: bfloat16 [262144, 1024], P('seq', 'ch'), may hold values from -6 to 6
- grad_out: bfloat16 [262144, 1024], P('seq', 'ch'), may hold values from -6 to 6
- forward_inner: bfloat16 [512, 512], replicated, may hold values from -0.25 to 0.25
- forward_outer: bfloat16 [512, 512], replicated, may hold values from -0.25 to 0.25
- inverse_outer: bfloat16 [512, 512], replicated, may hold values from -0.25 to 0.25
- inverse_inner: bfloat16 [512, 512], replicated, may hold values from -0.25 to 0.25
- twiddle_forward: float32 [512, 512], P(None, 'seq'), may hold values from 0.5 to 1.5
- twiddle_inverse: float32 [512, 512], P(None, 'seq'), may hold values from 0.5 to 1.5
- filter_in: float32 [32, 128], replicated, may hold values from -1 to 1
- filter_bias: float32 [128], replicated, may hold values from -3.140625 to 3.140625
- filter_out: bfloat16 [128, 1024], P(None, 'ch'), may hold values from -0.5 to 0.5
Outputs:
- grad_input: bfloat16 [262144, 1024], P('seq', 'ch')
- grad_gate: bfloat16 [262144, 1024], P('seq', 'ch')
- grad_filter_out: float32 [128, 1024], P(None, 'ch')
- grad_filter_in: float32 [32, 128], replicated
- grad_filter_bias: float32 [128], replicated
All inputs are finite; a program needn't handle non-finite values.
Results may differ from a plain program's by a relative error of at most 0.009.
Values may be sent and summed in bfloat16 or wider, within the bound.
No kernel may reach another device: no remote copies, remote signals or barrier semaphores. Data moves between devices by JAX's collectives and lax.ppermute only.
A program may use at most 128 MiB of HBM per device.

v0:
```python
import math

import jax
import jax.numpy as jnp
from jax import lax
from jax.sharding import PartitionSpec as P


def features(rows_index, cols_index, feature_count, size_a, size_b):
    halves = feature_count // 2
    series = jnp.arange(halves, dtype=jnp.int32)
    row_freq = (7 * series + 1) % size_a
    col_freq = (13 * series + 3) % size_b
    row_phase = (rows_index[:, None, None] * row_freq[None, None, :] % size_a).astype(
        jnp.float32
    ) / size_a
    col_phase = (cols_index[None, :, None] * col_freq[None, None, :] % size_b).astype(
        jnp.float32
    ) / size_b
    angles = 2.0 * math.pi * (row_phase + col_phase)
    return jnp.concatenate([jnp.sin(angles), jnp.cos(angles)], axis=-1)


def shards(
    gated_input,
    out_gate,
    grad_out,
    forward_inner,
    forward_outer,
    inverse_outer,
    inverse_inner,
    twiddle_forward,
    twiddle_inverse,
    filter_in,
    filter_bias,
    filter_out,
):
    highest = lax.Precision.HIGHEST
    size_a = forward_outer.shape[0]
    size_b = forward_inner.shape[0]
    local_rows = gated_input.shape[0] // size_b
    channels = gated_input.shape[1]
    local_cols = twiddle_forward.shape[1]
    inputs = gated_input.reshape(local_rows, size_b, channels)
    gates = out_gate.reshape(local_rows, size_b, channels)
    upstream = grad_out.reshape(local_rows, size_b, channels)
    first = jnp.einsum(
        "kb,abc->akc", forward_inner, inputs, preferred_element_type=jnp.float32
    ).astype(jnp.bfloat16)
    grad_mixed = (gates.astype(jnp.float32) * upstream.astype(jnp.float32)).astype(jnp.bfloat16)
    grad_back = jnp.einsum(
        "bk,abc->akc", inverse_inner, grad_mixed, preferred_element_type=jnp.float32
    ).astype(jnp.bfloat16)
    turned = (
        twiddle_forward[:, :, None]
        * lax.all_to_all(first, "seq", split_axis=1, concat_axis=0, tiled=True).astype(jnp.float32)
    ).astype(jnp.bfloat16)
    spectrum = jnp.einsum(
        "ja,akc->jkc", forward_outer, turned, preferred_element_type=jnp.float32
    ).astype(jnp.bfloat16)
    col_index = lax.axis_index("seq") * local_cols + jnp.arange(local_cols, dtype=jnp.int32)
    feature_map = features(
        jnp.arange(size_a, dtype=jnp.int32), col_index, filter_in.shape[0], size_a, size_b
    )
    preact = jnp.einsum("jke,eh->jkh", feature_map, filter_in, precision=highest) + filter_bias
    hidden = jnp.sin(preact).astype(jnp.bfloat16)
    kernel = jnp.einsum("jkh,hc->jkc", hidden, filter_out, preferred_element_type=jnp.float32)
    filtered = (kernel * spectrum.astype(jnp.float32)).astype(jnp.bfloat16)
    back = (
        twiddle_inverse[:, :, None]
        * jnp.einsum("aj,jkc->akc", inverse_outer, filtered, preferred_element_type=jnp.float32)
    ).astype(jnp.bfloat16)
    mixed = jnp.einsum(
        "bk,akc->abc",
        inverse_inner,
        lax.all_to_all(back, "seq", split_axis=0, concat_axis=1, tiled=True),
        preferred_element_type=jnp.float32,
    )
    turned_back = (
        twiddle_inverse[:, :, None]
        * lax.all_to_all(grad_back, "seq", split_axis=1, concat_axis=0, tiled=True).astype(
            jnp.float32
        )
    ).astype(jnp.bfloat16)
    grad_filtered = jnp.einsum(
        "aj,akc->jkc", inverse_outer, turned_back, preferred_element_type=jnp.float32
    )
    grad_kernel = (grad_filtered * spectrum.astype(jnp.float32)).astype(jnp.bfloat16)
    grad_spectrum = (grad_filtered * kernel).astype(jnp.bfloat16)
    grad_first = (
        twiddle_forward[:, :, None]
        * jnp.einsum(
            "ja,jkc->akc", forward_outer, grad_spectrum, preferred_element_type=jnp.float32
        )
    ).astype(jnp.bfloat16)
    grad_input = jnp.einsum(
        "kb,akc->abc",
        forward_inner,
        lax.all_to_all(grad_first, "seq", split_axis=0, concat_axis=1, tiled=True),
        preferred_element_type=jnp.float32,
    ).astype(jnp.bfloat16)
    grad_gate = (upstream.astype(jnp.float32) * mixed).astype(jnp.bfloat16)
    weight_grad = (
        jnp.einsum("jkh,jkc->hc", hidden, grad_kernel, preferred_element_type=jnp.float32) / size_a
    )
    hidden_part = jnp.einsum(
        "jkc,hc->jkh", grad_kernel, filter_out, preferred_element_type=jnp.float32
    )
    hidden_total = lax.psum(hidden_part, "ch")
    grad_preact = hidden_total * jnp.cos(preact)
    layer_grad = jnp.einsum("jke,jkh->eh", feature_map, grad_preact, precision=highest) / size_a
    bias_grad = jnp.sum(grad_preact, axis=(0, 1)) / size_a
    weight_grad, layer_grad, bias_grad = lax.psum((weight_grad, layer_grad, bias_grad), "seq")
    grad_input = grad_input.reshape(local_rows * size_b, channels)
    grad_gate = grad_gate.reshape(local_rows * size_b, channels)
    return (grad_input, grad_gate, weight_grad, layer_grad, bias_grad)


def solution(mesh):
    return jax.shard_map(
        shards,
        mesh=mesh,
        in_specs=(
            P("seq", "ch"),
            P("seq", "ch"),
            P("seq", "ch"),
            P(),
            P(),
            P(),
            P(),
            P(None, "seq"),
            P(None, "seq"),
            P(),
            P(),
            P(None, "ch"),
        ),
        out_specs=(P("seq", "ch"), P("seq", "ch"), P(None, "ch"), P(), P()),
        check_vma=False,
    )
```

profile of v0, /device:TPU:1, one launch (start us, length us, event | category | flops | bytes accessed | tf_op | source)
XLA Modules:
  0.0 625.7 jit_solution(3149607376151980880)
XLA Ops:
  7.2 0.0 copy-start
  7.2 1.6 copy-done
  8.8 3.7 convert_bitcast_fusion.2
  12.4 4.5 copy.60
  16.9 13.3 %all-to-all-start.2 = ((bf16[8,512,256]{2,0,1:T(8,128)(2,1)}), bf16[8,512,256]{2,0,1:T(8,128)(2,1)S(1)}, u32[]{:S(2)}, u32[]{:S(2)}) async-start(bf16[8,512,256]{2,0,1:T(8,128)(2,1)} %copy.60), calls=%async_computation.2 | async-start | bytes 4194304 | tf_op jit(solution)/shard_map/all_to_all | solution.py:56
  30.2 4.8 convert_bitcast_fusion.4
  35.1 4.5 copy.50
  39.6 41.9 %all-to-all-done.2 = bf16[8,512,256]{2,0,1:T(8,128)(2,1)S(1)} async-done(((bf16[8,512,256]{2,0,1:T(8,128)(2,1)}), bf16[8,512,256]{2,0,1:T(8,128)(2,1)S(1)}, u32[]{:S(2)}, u32[]{:S(2)}) %all-to-all-start.2) | async-done | bytes 2097184 | tf_op jit(solution)/shard_map/all_to_all | solution.py:56
  81.5 6.0 all-to-all-start
  87.5 0.2 all-reduce.6.cloned.1.call-start
  87.7 0.4 convert_bitcast_fusion
  88.1 2.6 copy.62
  90.7 5.3 copy.63
  96.1 42.6 %all-to-all-done = bf16[8,512,256]{2,0,1:T(8,128)(2,1)} async-done(((bf16[8,512,256]{2,0,1:T(8,128)(2,1)}), bf16[8,512,256]{2,0,1:T(8,128)(2,1)}, u32[]{:S(2)}, u32[]{:S(2)}) %all-to-all-start) | async-done | bytes 2097184 | tf_op jit(solution)/shard_map/all_to_all | solution.py:81
  138.6 2.0 convert_bitcast_fusion.1
  140.7 2.6 copy.52
  143.3 5.4 copy.53
  148.7 3.6 fusion.20
  152.3 1.2 fusion.7
  153.6 1.9 copy-done.2
  155.5 2.4 fusion.41
  158.0 0.0 all-reduce.6.cloned.1.call-update
  158.0 0.1 fusion.52
  158.1 0.1 fusion.46
  158.2 1.0 fusion.40
  159.2 59.2 %all-reduce.6.cloned.1.call-done = f32[512,8,128]{2,0,1:T(8,128)} async-done(((f32[512,8,128]{2,0,1:T(8,128)}), f32[512,8,128]{2,0,1:T(8,128)}) %all-reduce.6.cloned.1.call-update) | async-done | bytes 2097168 | tf_op jit(solution)/shard_map/psum | solution.py:109
  218.4 12.1 %fusion.28 = (f32[128]{0:T(128)S(1)}, f32[512,8,128]{2,0,1:T(8,128)S(1)}) fusion(f32[512,8,128]{2,0,1:T(8,128)} %all-reduce.6.cloned.1.call-done, f32[128]{0:T(128)S(1)} %copy-done.15, f32[32,128]{1,0:T(8,128)S(1)} %copy-done.14, f32[512,8,16]{0,2,1:T(8,128)S(1)} %get-tuple-element.8, f32[512,8,16]{0,2,1:T(8,128)S(1)} %get-tuple-element.7), kind=kOutput, calls=%fused_computation.39 | convolution fusion | flops 203030400 | bytes 4736000 | tf_op jit(solution)/shard_map/jke,eh->jkh/dot_general | solution.py:65
  230.5 1.3 copy-done.4
  231.8 8.5 %fusion.38 = f32[512,8,256]{0,2,1:T(8,128)S(1)} fusion(f32[512,8,128]{2,0,1:T(8,128)S(1)} %get-tuple-element.10, f32[128]{0:T(128)S(1)} %copy-done.15, bf16[128,256]{1,0:T(8,128)(2,1)S(1)} %copy-done.11), kind=kOutput, calls=%fused_computation.50 | convolution fusion | flops 269484032 | bytes 6357504 | tf_op jit(solution)/shard_map/jkh,hc->jkc/dot_general | solution.py:67
  240.3 2.0 copy-done.3
  242.3 2.6 fusion.2
  244.9 4.5 copy.65
  249.4 11.0 %all-to-all-start.3 = ((bf16[512,8,256]{2,1,0:T(8,128)(2,1)}), bf16[512,8,256]{2,1,0:T(8,128)(2,1)}, u32[]{:S(2)}, u32[]{:S(2)}) async-start(bf16[512,8,256]{2,1,0:T(8,128)(2,1)} %copy.65), calls=%async_computation.3 | async-start | bytes 4194304 | tf_op jit(solution)/shard_map/all_to_all | solution.py:76
  260.5 6.0 fusion.5
  266.5 4.5 copy.55
  271.0 40.6 %all-to-all-done.3 = bf16[512,8,256]{2,1,0:T(8,128)(2,1)} async-done(((bf16[512,8,256]{2,1,0:T(8,128)(2,1)}), bf16[512,8,256]{2,1,0:T(8,128)(2,1)}, u32[]{:S(2)}, u32[]{:S(2)}) %all-to-all-start.3) | async-done | bytes 2097184 | tf_op jit(solution)/shard_map/all_to_all | solution.py:76
  311.6 6.0 all-to-all-start.1
  317.6 0.0 all-reduce.4.cloned.1.call-start
  317.7 4.2 copy.68
  321.9 10.1 %fusion.25 = f32[128,256]{1,0:T(8,128)} fusion(f32[512,8,128]{2,0,1:T(8,128)} %copy-done.4, f32[128]{0:T(128)S(1)} %copy-done.15, bf16[8,256,512]{2,1,0:T(8,128)(2,1)S(1)} %fusion.20, f32[8,256,512]{2,1,0:T(8,128)} %copy-done.2), kind=kOutput, calls=%fused_computation.35 | convolution fusion | flops 272662528 | bytes 8520192 | tf_op jit(solution)/shard_map/jkh,jkc->hc/dot_general | solution.py:104
  332.0 0.0 all-reduce.4.cloned.1.call-update
  332.0 9.6 %fusion.26 = f32[32,128]{1,0:T(8,128)S(1)} fusion(f32[512,8,128]{2,0,1:T(8,128)} %all-reduce.6.cloned.1.call-done, f32[512,8,128]{2,0,1:T(8,128)} %copy-done.4, f32[128]{0:T(128)S(1)} %copy-done.15, f32[512,8,16]{0,2,1:T(8,128)S(1)} %get-tuple-element.8, f32[512,8,16]{0,2,1:T(8,128)S(1)} %get-tuple-element.7), kind=kOutput, calls=%fused_computation.37 | convolution fusion | flops 202510336 | bytes 4735488 | tf_op jit(solution)/shard_map/jke,jkh->eh/dot_general | solution.py:111
  341.7 257.9 %all-reduce = (f32[32,128]{1,0:T(8,128)}, f32[128]{0:T(128)}) all-reduce(f32[32,128]{1,0:T(8,128)S(1)} %fusion.26, f32[128]{0:T(128)S(1)} %broadcast_multiply_fusion), channel_id=1, replica_groups=mesh['seq'=64,'ch'=4] {'seq'}, use_global_device_ids=true, to_apply=%region_2.3 | all-reduce | flops 4224 | bytes 33792 | tf_op jit(solution)/shard_map/psum | solution.py:113
  599.6 5.5 fusion.1
  605.1 4.2 convert_bitcast_fusion.3
  609.3 4.1 copy.58
  613.3 3.9 copy.69
  617.3 1.6 copy.95
  (35 shorter events, 0.1 us)
Async XLA Ops:
  7.2 1.6 copy-start
  16.9 13.3 %copy-start.9 = (bf16[512,512]{1,0:T(8,128)(2,1)S(1)}, bf16[512,512]{1,0:T(8,128)(2,1)}, u32[]{:S(2)}) copy-start(bf16[512,512]{1,0:T(8,128)(2,1)} %param.18) | copy-start | bytes 1572868
  16.9 64.5 %all-to-all-start.2 = ((bf16[8,512,256]{2,0,1:T(8,128)(2,1)}), bf16[8,512,256]{2,0,1:T(8,128)(2,1)S(1)}, u32[]{:S(2)}, u32[]{:S(2)}) async-start(bf16[8,512,256]{2,0,1:T(8,128)(2,1)} %copy.60), calls=%async_computation.2 | async-start | bytes 4194304 | tf_op jit(solution)/shard_map/all_to_all | solution.py:56
  81.5 57.2 %all-to-all-start = ((bf16[8,512,256]{2,0,1:T(8,128)(2,1)}), bf16[8,512,256]{2,0,1:T(8,128)(2,1)}, u32[]{:S(2)}, u32[]{:S(2)}) async-start(bf16[8,512,256]{2,0,1:T(8,128)(2,1)} %copy.50), calls=%async_computation | async-start | bytes 4194304 | tf_op jit(solution)/shard_map/all_to_all | solution.py:81
  87.5 130.9 %all-reduce.6.cloned.1.call-start = ((), (), s32[]{:S(2)}) async-start(), calls=%async_computation.5 | async-start | bytes 4194304 | tf_op jit(solution)/shard_map/psum | solution.py:109
  143.3 5.4 copy-start.7
  143.3 5.4 copy-start.13
  148.6 3.7 copy-start.5
  148.6 3.7 copy-start.6
  148.7 3.7 copy-start.12
  152.3 3.2 copy-start.11
  153.6 1.9 copy-start.2
  158.0 60.4 %copy-start.14 = (f32[32,128]{1,0:T(8,128)S(1)}, f32[32,128]{1,0:T(8,128)}, u32[]{:S(2)}) copy-start(f32[32,128]{1,0:T(8,128)} %param.21) | copy-start | bytes 49156
  158.0 60.4 %copy-start.15 = (f32[128]{0:T(128)S(1)}, f32[128]{0:T(128)}, u32[]{:S(2)}) copy-start(f32[128]{0:T(128)} %param.22) | copy-start | bytes 1540
  230.5 1.3 copy-start.4
  240.3 2.0 copy-start.3
  249.4 11.0 %copy-start.8 = (bf16[512,512]{1,0:T(8,128)(2,1)S(1)}, bf16[512,512]{1,0:T(8,128)(2,1)}, u32[]{:S(2)}) copy-start(bf16[512,512]{1,0:T(8,128)(2,1)} %param.16) | copy-start | bytes 1572868
  249.4 62.2 %all-to-all-start.3 = ((bf16[512,8,256]{2,1,0:T(8,128)(2,1)}), bf16[512,8,256]{2,1,0:T(8,128)(2,1)}, u32[]{:S(2)}, u32[]{:S(2)}) async-start(bf16[512,8,256]{2,1,0:T(8,128)(2,1)} %copy.65), calls=%async_computation.3 | async-start | bytes 4194304 | tf_op jit(solution)/shard_map/all_to_all | solution.py:76
  311.6 293.5 %all-to-all-start.1 = ((bf16[512,8,256]{2,1,0:T(8,128)(2,1)}), bf16[512,8,256]{2,1,0:T(8,128)(2,1)}, u32[]{:S(2)}, u32[]{:S(2)}) async-start(bf16[512,8,256]{2,1,0:T(8,128)(2,1)} %copy.55), calls=%async_computation.1 | async-start | bytes 4194304 | tf_op jit(solution)/shard_map/all_to_all | solution.py:99
  317.6 299.6 %all-reduce.4.cloned.1.call-start = ((), (), s32[]{:S(2)}) async-start(), calls=%async_computation.4 | async-start | bytes 262144 | tf_op jit(solution)/shard_map/psum | solution.py:113
  332.0 267.6 %copy-start.10 = (bf16[512,512]{1,0:T(8,128)(2,1)S(1)}, bf16[512,512]{1,0:T(8,128)(2,1)}, u32[]{:S(2)}) copy-start(bf16[512,512]{1,0:T(8,128)(2,1)} %param.18) | copy-start | bytes 1572868
  599.6 5.5 copy-start.16
  609.3 9.5 %copy-start.1 = (bf16[4096,256]{1,0:T(8,128)(2,1)S(1)}, bf16[4096,256]{1,0:T(8,128)(2,1)}, u32[]{:S(2)}) copy-start(bf16[4096,256]{1,0:T(8,128)(2,1)} %param.12) | copy-start | bytes 6291460
Sparse Core Ops, SparseCore 0:
  158.1 60.2 all-reduce.5
  332.1 177.9 all-reduce.3
where the time goes:
time: 630 us; the launch traced here: 626 us
  blocking collectives  258 us (41%)
  waiting for transfers between devices  184 us (29%)
  matrix products  74.5 us (12%)
  local copies, waits for them, and re-layouts  54.5 us (9%)
  starting transfers between devices  36.6 us (6%)
  between operations  14.3 us (2%)
    psum x1, blocking collectives, shards(): lax.psum((weight_grad, layer_grad, bias_grad), 'seq')  258 us
    psum x1, waiting for transfers between devices, shards(): hidden_total = lax.psum(hidden_part, 'ch')  59.2 us
    all_to_all x1, waiting for transfers between devices, shards(): lax.all_to_all(grad_back, 'seq', split_axis=1, concat_axis=0, tiled=True)  42.6 us
    all_to_all x1, waiting for transfers between devices, shards(): lax.all_to_all(first, 'seq', split_axis=1, concat_axis=0, tiled=True)  41.9 us
    all_to_all x1, waiting for transfers between devices, shards(): lax.all_to_all(back, 'seq', split_axis=0, concat_axis=1, tiled=True)  40.6 us
    all_to_all x1, starting transfers between devices, shards(): lax.all_to_all(first, 'seq', split_axis=1, concat_axis=0, tiled=True)  13.3 us
  transfers between devices with their start and end apart: 6, of which 4 were waited for; matrix products, arithmetic and copies ran while one was open for 11% of the time, Pallas kernels for 0%

commit v1 on v0

v1 whole, which is shorter than its diff:
```python
import functools
import math

import jax
import jax.numpy as jnp
import numpy as np
from jax import lax
from jax.experimental import pallas as pl
from jax.experimental.pallas import tpu as pltpu
from jax.sharding import PartitionSpec as P

F32 = jnp.float32
BF16 = jnp.bfloat16
MIB = 1 << 20
PARTS = 64
ROWS = 8
OUTER_LIMIT = 40
CHUNKS = 4
TABLE = 40


def dot(x, y, precision=None):
    return lax.dot_general(
        x, y, (((1,), (0,)), ((), ())), precision=precision, preferred_element_type=F32
    )


def full(shape, buffers=1):
    return pl.BlockSpec(
        shape, lambda *_: (0,) * len(shape), pipeline_mode=pl.Buffered(buffers)
    )


def outer_table(size, halves):
    series = np.arange(halves)
    phase = (np.arange(size)[:, None] * ((7 * series + 1) % size)[None, :]) % size
    angles = 2.0 * np.pi * phase / size
    table = np.zeros((size, TABLE), np.float32)
    table[:, :halves] = np.sin(angles)
    table[:, halves : 2 * halves] = np.cos(angles)
    table[:, 2 * halves] = 1.0
    return table


def inner_kernel(u_hbm, g_hbm, dy_hbm, fi_hbm, ii_hbm, o_hbm, u_ref, g_ref, dy_ref, fi_ref, ii_ref, o_ref, in_sem, out_sem):
    size, channels = u_ref.shape[1:]
    pairs = ROWS // 2
    copies = {}

    def fetch(key, source, target):
        copies[key] = pltpu.make_async_copy(source, target, in_sem.at[len(copies)])
        copies[key].start()

    fetch("fi", fi_hbm, fi_ref)
    for p in range(pairs):
        at = pl.ds(2 * p, 2)
        fetch(("u", p), u_hbm.at[at], u_ref.at[at])
    fetch("ii", ii_hbm, ii_ref)
    for p in range(pairs):
        at = pl.ds(2 * p, 2)
        fetch(("g", p), g_hbm.at[at], g_ref.at[at])
        fetch(("dy", p), dy_hbm.at[at], dy_ref.at[at])

    sends = []

    def emit(which, p, matrix, blocks):
        at = pl.ds(2 * ROWS * p, 2 * ROWS)
        parts = [dot(matrix, block).reshape(PARTS, 1, ROWS, channels) for block in blocks]
        value = jnp.concatenate(parts, 1).reshape(PARTS, 2 * ROWS, channels).astype(BF16)
        o_ref[:, which, 2 * ROWS * p : 2 * ROWS * (p + 1), :] = value
        sends.append(pltpu.make_async_copy(o_ref.at[:, which, at, :], o_hbm.at[:, which, at, :], out_sem.at[len(sends)]))
        sends[-1].start()

    copies["fi"].wait()
    for p in range(pairs):
        copies["u", p].wait()
        emit(0, p, fi_ref[...], [u_ref[2 * p], u_ref[2 * p + 1]])
    copies["ii"].wait()
    turned = ii_ref[...].astype(F32).T.astype(BF16)
    for p in range(pairs):
        copies["g", p].wait()
        copies["dy", p].wait()
        mixed = [
            (g_ref[i].astype(F32) * dy_ref[i].astype(F32)).astype(BF16)
            for i in (2 * p, 2 * p + 1)
        ]
        emit(1, p, turned, mixed)
    for send in sends:
        send.wait()


def filter_kernel(col_ref, tab_ref, fin_ref, bias_ref, hid_ref, hidt_ref, cos_ref, q_ref):
    step = pl.program_id(0)
    size = tab_ref.shape[0]
    hidden = bias_ref.shape[1]
    halves = fin_ref.shape[0] // 2
    col = col_ref[0] + step
    series = lax.broadcasted_iota(jnp.int32, (halves, hidden), 0)
    phase = (((13 * series + 3) % size) * col) % size
    angle = phase.astype(F32) * (2.0 * math.pi / size)
    sq, cq = jnp.sin(angle), jnp.cos(angle)
    q_ref[0, :halves] = cq
    q_ref[0, halves:] = sq
    ws, wc = fin_ref[:halves], fin_ref[halves:]
    weights = jnp.concatenate(
        [
            cq * ws - sq * wc,
            sq * ws + cq * wc,
            bias_ref[...],
            jnp.zeros((TABLE - 2 * halves - 1, hidden), F32),
        ],
        0,
    )
    preact = dot(tab_ref[...], weights, lax.Precision.HIGHEST)
    value = jnp.sin(preact)
    hid_ref[0] = value.astype(BF16)
    hidt_ref[0] = value.T.astype(BF16)
    cos_ref[0] = jnp.cos(preact)


def outer_kernel(
    r_hbm, fo_ref, fot_ref, io_ref, iot_ref, w_ref, wt_ref, tabt_ref, tf_ref, ti_ref,
    hid_hbm, hidt_hbm, cos_hbm, q_ref,
    o_hbm, s_ref, x_ref, y_ref, wire_ref, hid_ref, hidt_ref, cos_ref, in_sem, gen_sem, out_sem,
):
    size = fo_ref.shape[0]
    hidden, channels = w_ref.shape
    lanes = x_ref.shape[2]
    halves = q_ref.shape[1] // 2
    rows = wire_ref.shape[2]
    split = channels // lanes
    chunk = PARTS // CHUNKS

    def moved(source, target, sem):
        copies = []
        for which in (0, 1):
            for c in range(CHUNKS):
                at = pl.ds(c * chunk, chunk)
                copies.append(pltpu.make_async_copy(source.at[at, which], target.at[at, which], sem.at[len(copies)]))
        return copies

    loads = moved(r_hbm, wire_ref, in_sem)
    for load in loads:
        load.start()
    generated = [
        pltpu.make_async_copy(source, target, gen_sem.at[i])
        for i, (source, target) in enumerate(((hid_hbm, hid_ref), (hidt_hbm, hidt_ref), (cos_hbm, cos_ref)))
    ]
    for copy in generated:
        copy.start()

    for which, ref in ((0, x_ref), (1, y_ref)):
        for c in range(CHUNKS):
            loads[which * CHUNKS + c].wait()
            for part in range(c * chunk, (c + 1) * chunk):
                for i in range(split):
                    ref[i, part * rows : (part + 1) * rows] = wire_ref[part, which, :, i * lanes : (i + 1) * lanes].astype(F32)
    for copy in generated:
        copy.wait()

    weight = jnp.zeros((hidden, channels), F32)
    layer = [jnp.zeros((halves, hidden), F32)] * 2
    bias = jnp.zeros((TABLE - 2 * halves, hidden), F32)
    pending = []
    for k in range(ROWS):
        mine = pl.ds(k, size, stride=ROWS)
        tf = jnp.broadcast_to(tf_ref[:, k : k + 1], (size, lanes))
        ti = jnp.broadcast_to(ti_ref[:, k : k + 1], (size, lanes))

        def load(ref, scale):
            return jnp.concatenate([(scale * ref[i, mine, :]).astype(BF16) for i in range(split)], 1)

        def store(ref, scale, value):
            for i in range(split):
                ref[i, mine, :] = scale * value[:, i * lanes : (i + 1) * lanes]

        spectrum = dot(fo_ref[...], load(x_ref, tf)).astype(BF16).astype(F32)
        grad_filtered = dot(iot_ref[...], load(y_ref, ti))
        kernel = dot(hid_ref[k], w_ref[...])
        store(x_ref, ti, dot(io_ref[...], (kernel * spectrum).astype(BF16)))
        store(y_ref, tf, dot(fot_ref[...], (grad_filtered * kernel).astype(BF16)))
        grad_kernel = (grad_filtered * spectrum).astype(BF16)
        weight = weight + dot(hidt_ref[k], grad_kernel)
        pending.append(dot(grad_kernel, wt_ref[...]) * cos_ref[k])
        if len(pending) == 2:
            grad_preact = jnp.concatenate(pending, 1)
            pending = []
            high = grad_preact.astype(BF16)
            low = (grad_preact - high.astype(F32)).astype(BF16)
            upper = dot(tabt_ref[...], high)
            moments = upper[:TABLE] + upper[TABLE:] + dot(tabt_ref[...], low)[:TABLE]
            for i in range(2):
                part = moments[:, i * hidden : (i + 1) * hidden]
                cq, sq = q_ref[k - 1 + i, :halves], q_ref[k - 1 + i, halves:]
                ms, mc = part[:halves], part[halves : 2 * halves]
                layer = [layer[0] + cq * ms + sq * mc, layer[1] + cq * mc - sq * ms]
                bias = bias + part[2 * halves :]

    sends = moved(wire_ref, o_hbm, out_sem)
    for which, ref in ((0, x_ref), (1, y_ref)):
        for c in range(CHUNKS):
            for part in range(c * chunk, (c + 1) * chunk):
                for i in range(split):
                    wire_ref[part, which, :, i * lanes : (i + 1) * lanes] = ref[i, part * rows : (part + 1) * rows].astype(BF16)
            sends[which * CHUNKS + c].start()

    scale = 1.0 / size
    for i in range(split):
        s_ref[i * hidden : (i + 1) * hidden] = weight[:, i * lanes : (i + 1) * lanes] * scale
    s_ref[split * hidden :] = jnp.concatenate(layer + [bias], 0) * scale
    for send in sends:
        send.wait()


def tokens_kernel(x_hbm, dy_ref, ii_ref, fi_ref, gi_hbm, gg_hbm, x_ref, gi_ref, gg_ref, in_sem, out_sem):
    size, channels = dy_ref.shape[1:]
    pairs = ROWS // 2
    loads, sends = {}, []
    for which in (0, 1):
        for p in range(pairs):
            at = pl.ds(2 * ROWS * p, 2 * ROWS)
            loads[which, p] = pltpu.make_async_copy(x_hbm.at[:, which, at, :], x_ref.at[:, which, at, :], in_sem.at[len(loads)])
            loads[which, p].start()

    def operands(which, p):
        loads[which, p].wait()
        value = x_ref[:, which, 2 * ROWS * p : 2 * ROWS * (p + 1), :].astype(F32)
        return [value[:, i * ROWS : (i + 1) * ROWS].reshape(size, channels).astype(BF16) for i in range(2)]

    def emit(source, target, p):
        at = pl.ds(2 * p, 2)
        sends.append(pltpu.make_async_copy(source.at[at], target.at[at], out_sem.at[len(sends)]))
        sends[-1].start()

    for p in range(pairs):
        for i, back in enumerate(operands(0, p)):
            mixed = dot(ii_ref[...], back)
            gg_ref[2 * p + i] = (dy_ref[2 * p + i].astype(F32) * mixed).astype(BF16)
        emit(gg_ref, gg_hbm, p)
    turned = fi_ref[...].astype(F32).T.astype(BF16)
    for p in range(pairs):
        for i, first in enumerate(operands(1, p)):
            gi_ref[2 * p + i] = dot(turned, first).astype(BF16)
        emit(gi_ref, gi_hbm, p)
    for send in sends:
        send.wait()


def pair_kernel(one_ref, other_ref, after_ref, o_ref):
    o_ref[...] = one_ref[...] + other_ref[...]


def finish_kernel(v_ref, a_ref, b_ref, c_ref, after_ref, w_ref, l_ref, b_out_ref):
    hidden, channels = w_ref.shape
    features = l_ref.shape[0]
    lanes = v_ref.shape[1]
    total = (v_ref[...] + a_ref[...]) + (b_ref[...] + c_ref[...])
    split = channels // lanes
    for i in range(split):
        w_ref[:, i * lanes : (i + 1) * lanes] = total[i * hidden : (i + 1) * hidden]
    l_ref[...] = total[split * hidden : split * hidden + features]
    b_out_ref[...] = total[split * hidden + features : split * hidden + features + 1]


def params(limit, axes=1):
    return pltpu.CompilerParams(
        vmem_limit_bytes=limit * MIB, dimension_semantics=("arbitrary",) * axes
    )


def exchanged(value, axis, count, step):
    return lax.ppermute(value, axis, [(i, i ^ step) for i in range(count)])


def doubled(value, axis, count, steps):
    for step in steps:
        value = value + exchanged(value, axis, count, step)
    return value


def shards(
    gated_input,
    out_gate,
    grad_out,
    forward_inner,
    forward_outer,
    inverse_outer,
    inverse_inner,
    twiddle_forward,
    twiddle_inverse,
    filter_in,
    filter_bias,
    filter_out,
):
    size = forward_outer.shape[0]
    channels = gated_input.shape[1]
    hidden = filter_in.shape[1]
    features = filter_in.shape[0]
    lanes = 128
    tokens = (ROWS, size, channels)
    inputs, gates, upstream = (x.reshape(tokens) for x in (gated_input, out_gate, grad_out))
    square = (size, size)
    pair = pl.BlockSpec((2, size, channels), lambda p: (p, 0, 0))
    wire = (PARTS, 2, ROWS * ROWS, channels)
    wire_pair = pl.BlockSpec((PARTS, 2, 2 * ROWS, channels), lambda p: (0, 0, p, 0))

    anywhere = pl.BlockSpec(memory_space=pltpu.HBM)
    inside = pl.BlockSpec(memory_space=pltpu.VMEM)
    sent = pl.pallas_call(
        inner_kernel,
        out_shape=jax.ShapeDtypeStruct(wire, BF16),
        in_specs=[anywhere] * 5,
        out_specs=anywhere,
        scratch_shapes=[pltpu.VMEM(tokens, BF16)] * 3
        + [pltpu.VMEM(square, BF16)] * 2
        + [pltpu.VMEM(wire, BF16), pltpu.SemaphoreType.DMA((2 + 3 * ROWS // 2,)), pltpu.SemaphoreType.DMA((ROWS,))],
        compiler_params=pltpu.CompilerParams(vmem_limit_bytes=62 * MIB),
        cost_estimate=pl.CostEstimate(flops=4 * ROWS * size * size * channels, bytes_accessed=10 * MIB, transcendentals=0),
        name="inner_transforms",
    )(inputs, gates, upstream, forward_inner, inverse_inner)

    column = lax.axis_index("seq").astype(jnp.int32).reshape(1) * ROWS
    sent, column = lax.optimization_barrier((sent, column))
    received = lax.all_to_all(sent, "seq", split_axis=0, concat_axis=0, tiled=True)

    table = outer_table(size, features // 2)
    each = lambda *shape: pl.BlockSpec((1,) + shape, lambda k, *_: (k,) + (0,) * len(shape))
    made = [
        ((size, hidden), BF16),
        ((hidden, size), BF16),
        ((size, hidden), F32),
        ((features, hidden), F32),
    ]
    generated = pl.pallas_call(
        filter_kernel,
        grid_spec=pltpu.PrefetchScalarGridSpec(
            num_scalar_prefetch=1,
            grid=(ROWS,),
            in_specs=[full((size, TABLE)), full((features, hidden)), full((1, hidden))],
            out_specs=[each(*shape) for shape, _ in made],
        ),
        out_shape=[jax.ShapeDtypeStruct((ROWS,) + shape, kind) for shape, kind in made],
        compiler_params=params(32),
        cost_estimate=pl.CostEstimate(flops=40 * MIB, bytes_accessed=9 * MIB, transcendentals=2 * MIB),
        name="filter_generator",
    )(column, table, filter_in, filter_bias.reshape(1, hidden))

    small = (2 * hidden + TABLE, lanes)
    high = table.T.astype(BF16)
    low = (table.T - high.astype(np.float32)).astype(BF16)
    returned, partial = pl.pallas_call(
        outer_kernel,
        out_shape=[jax.ShapeDtypeStruct(wire, BF16), jax.ShapeDtypeStruct(small, F32)],
        in_specs=[anywhere] + [inside] * 9 + [anywhere] * 3 + [inside],
        out_specs=[anywhere, inside],
        scratch_shapes=[pltpu.VMEM((channels // lanes, ROWS * size, lanes), F32)] * 2
        + [pltpu.VMEM(wire, BF16)]
        + [pltpu.VMEM((ROWS,) + shape, kind) for shape, kind in made[:3]]
        + [pltpu.SemaphoreType.DMA((count,)) for count in (2 * CHUNKS, 3, 2 * CHUNKS)],
        compiler_params=pltpu.CompilerParams(vmem_limit_bytes=OUTER_LIMIT * MIB),
        cost_estimate=pl.CostEstimate(flops=10 * ROWS * size * size * channels, bytes_accessed=18 * MIB, transcendentals=0),
        name="outer_transforms",
    )(received, forward_outer, forward_outer.T, inverse_outer, inverse_outer.T, filter_out, filter_out.T, np.concatenate([high, low], 0), twiddle_forward, twiddle_inverse, *generated)

    arrived = lax.all_to_all(returned, "seq", split_axis=0, concat_axis=0, tiled=True)

    layer = doubled(partial[2 * hidden :], "ch", 4, (1, 2))
    total = jnp.concatenate([partial[: 2 * hidden], layer], 0)
    total = doubled(total, "seq", PARTS, (1, 16, 32))
    total = pl.pallas_call(
        pair_kernel,
        out_shape=jax.ShapeDtypeStruct(small, F32),
        in_specs=[inside, inside, anywhere],
        out_specs=inside,
        name="pair_sum",
    )(total, exchanged(total, "seq", PARTS, 2), arrived)
    others = [exchanged(total, "seq", PARTS, step) for step in (4, 8, 12)]

    grad_input, grad_gate = pl.pallas_call(
        tokens_kernel,
        out_shape=[jax.ShapeDtypeStruct(tokens, BF16)] * 2,
        in_specs=[anywhere, inside, inside, inside],
        out_specs=[anywhere] * 2,
        scratch_shapes=[pltpu.VMEM(wire, BF16), pltpu.VMEM(tokens, BF16), pltpu.VMEM(tokens, BF16), pltpu.SemaphoreType.DMA((ROWS,)), pltpu.SemaphoreType.DMA((ROWS,))],
        compiler_params=pltpu.CompilerParams(vmem_limit_bytes=32 * MIB),
        cost_estimate=pl.CostEstimate(flops=4 * ROWS * size * size * channels, bytes_accessed=10 * MIB, transcendentals=0),
        name="token_gradients",
    )(arrived, upstream, inverse_inner, forward_inner)
    weight_grad, layer_grad, bias_grad = pl.pallas_call(
        finish_kernel,
        out_shape=[
            jax.ShapeDtypeStruct((hidden, channels), F32),
            jax.ShapeDtypeStruct((features, hidden), F32),
            jax.ShapeDtypeStruct((1, hidden), F32),
        ],
        in_specs=[inside] * 4 + [anywhere],
        name="weight_gradients",
    )(total, *others, grad_gate)
    flat = (ROWS * size, channels)
    return grad_input.reshape(flat), grad_gate.reshape(flat), weight_grad, layer_grad, bias_grad.reshape(hidden)


def solution(mesh):
    return jax.shard_map(
        shards,
        mesh=mesh,
        in_specs=(
            P("seq", "ch"),
            P("seq", "ch"),
            P("seq", "ch"),
            P(),
            P(),
            P(),
            P(),
            P(None, "seq"),
            P(None, "seq"),
            P(),
            P(),
            P(None, "ch"),
        ),
        out_specs=(P("seq", "ch"), P("seq", "ch"), P(None, "ch"), P(), P()),
        check_vma=False,
    )
```

time: 630 us -> 261 us (0.41)
  blocking collectives: 258 us -> 0 us
  matrix products: 74.5 us -> 0 us
  local copies, waits for them, and re-layouts: 54.5 us -> 10.3 us
  Pallas kernels: 0 us -> 38.8 us
  between operations: 14.3 us -> 0.93 us
  waiting for transfers between devices: 184 us -> 174 us
    psum x1 -> x0, blocking collectives: 258 us -> none  [shards(): lax.psum((weight_grad, layer_grad, bias_grad), 'seq')]
    ppermute x0 -> x9, waiting for transfers between devices: none -> 91.6 us  [exchanged(): return lax.ppermute(value, axis, [(i, i ^ step) for i in range(count)])]
    dot_general x13 -> x0, matrix products: 74.5 us -> none  [the longest x1 12.1 us: shards(): jnp.einsum('jke,eh->jkh', feature_map, filter_in, precision=highest)]
    psum x2 -> x0, waiting for transfers between devices: 59.2 us -> none  [the longest x1 59.2 us: shards(): hidden_total = lax.psum(hidden_part, 'ch')]
    convert_element_type x11 -> x0, local copies, waits for them, and re-layouts: 46.1 us -> none  [the longest x2 7.96 us: shards(): lax.all_to_all(grad_back, 'seq', split_axis=1, concat_axis=0, tiled=True)]
    all_to_all x4 -> x2, waiting for transfers between devices: 125 us -> 81.9 us  [the longest x1 80.7 us: shards(): lax.all_to_all(sent, 'seq', split_axis=0, concat_axis=0, tiled=True)]
    pallas_call x0 -> x6, Pallas kernels: none -> 38.8 us  [the longest x1 12.7 us: shards(): pl.pallas_call(outer_kernel, out_shape=[jax.ShapeDtypeStruct(wire, BF16),...]
    ppermute x0 -> x9, starting transfers between devices: none -> 17.7 us  [exchanged(): return lax.ppermute(value, axis, [(i, i ^ step) for i in range(count)])]
  transfers between devices with their start and end apart: 6 -> 11, of which waited for: 4 -> 10; matrix products, arithmetic and copies ran while one was open for 11% -> 0% of each run, Pallas kernels for 0% -> 6%
where the time goes in v1:
time: 261 us
  waiting for transfers between devices  174 us (67%)
  Pallas kernels  38.8 us (15%)
  starting transfers between devices  37.1 us (14%)
  local copies, waits for them, and re-layouts  10.3 us (4%)
    ppermute x9, waiting for transfers between devices, exchanged(): return lax.ppermute(value, axis, [(i, i ^ step) for i in range(count)])  91.6 us
    all_to_all x1, waiting for transfers between devices, shards(): lax.all_to_all(sent, 'seq', split_axis=0, concat_axis=0, tiled=True)  80.7 us
    ppermute x9, starting transfers between devices, exchanged(): return lax.ppermute(value, axis, [(i, i ^ step) for i in range(count)])  17.7 us
    all_to_all x1, starting transfers between devices, shards(): lax.all_to_all(sent, 'seq', split_axis=0, concat_axis=0, tiled=True)  13.5 us
    pallas_call x1, Pallas kernels, shards(): pl.pallas_call(outer_kernel, out_shape=[jax.ShapeDtypeStruct(wire, BF16),...  12.7 us
    pallas_call x1, Pallas kernels, shards(): pl.pallas_call(filter_kernel, grid_spec=pltpu.PrefetchScalarGridSpec(num_...  10.8 us
    unnamed x51, local copies, waits for them, and re-layouts  10.3 us
    pallas_call x1, Pallas kernels, shards(): pl.pallas_call(inner_kernel, out_shape=jax.ShapeDtypeStruct(wire, BF16),...  6.2 us
  transfers between devices with their start and end apart: 11, of which 10 were waited for; matrix products, arithmetic and copies ran while one was open for 0% of the time, Pallas kernels for 6%

profile of v1, /device:TPU:1, one launch (start us, length us, event | category | flops | bytes accessed | tf_op | source)
XLA Modules:
  0.0 260.7 jit_solution(305919294618729357)
XLA Ops:
  0.6 6.2 %inner_transforms.1 = bf16[64,2,64,256]{3,2,1,0:T(8,128)(2,1)} custom-call(bf16[8,512,256]{2,1,0:T(8,128)(2,1)} %bitcast.18, bf16[8,512,256]{2,1,0:T(8,128)(2,1)} %bitcast.19, bf16[8,512,256]{2,1,0:T(8,128)(2,1)} %bitcast.11, bf16[512,512]{1,0:T(8,128)(2,1)} %fi_ref.1, bf16[512,512]{1,0:T(8,128)(2,1)} %ii_ref.1), custom_call_target="tpu_custom_call" | custom-call | flops 2147483648 | bytes 10485760 | tf_op jit(solution)/shard_map/inner_transforms/pallas_call | solution.py:309
  6.8 0.0 copy-start.6
  6.9 0.0 copy-start.4
  6.9 0.0 copy-start.5
  6.9 13.5 %all-to-all-start = ((bf16[64,2,64,256]{3,2,1,0:T(8,128)(2,1)}), bf16[64,2,64,256]{3,2,1,0:T(8,128)(2,1)}, u32[]{:S(2)}, u32[]{:S(2)}) async-start(bf16[64,2,64,256]{3,2,1,0:T(8,128)(2,1)} %inner_transforms.1), calls=%async_computation | async-start | bytes 8388608 | tf_op jit(solution)/shard_map/all_to_all | solution.py:324
  20.4 0.0 copy-start.8
  20.4 0.0 copy-start.9
  20.5 0.1 copy.21
  20.6 0.1 copy.22.tf_ref
  20.7 0.1 copy.23.ti_ref
  20.9 0.2 copy.19
  21.1 0.2 copy.20
  21.3 0.0 copy-start.10
  21.3 0.1 copy-done.9
  21.4 10.8 %filter_generator.1 = (bf16[8,512,128]{2,1,0:T(8,128)(2,1)S(1)}, bf16[8,128,512]{2,1,0:T(8,128)(2,1)S(1)}, f32[8,512,128]{2,1,0:T(8,128)S(1)}, f32[8,32,128]{2,1,0:T(8,128)S(1)}) custom-call(s32[1]{0:T(128)} %bitcast.3.col_ref, f32[512,40]{1,0:T(8,128)S(1)} %copy-done.9, f32[32,128]{1,0:T(8,128)S(1)} %copy-done.7, f32[1,128]{1,0:T(1,128)S(1)} %bitcast.16), custom_call_target="tpu_custom_call" | custom-call | flops 41943040 | bytes 9437184 | tf_op jit(solution)/shard_map/filter_generator/pallas_call | solution.py:334
  32.3 1.3 copy-done.11
  33.6 1.0 copy-done.13
  34.5 1.0 copy-done.15
  35.5 80.7 %all-to-all-done.r_hbm = bf16[64,2,64,256]{3,2,1,0:T(8,128)(2,1)} async-done(((bf16[64,2,64,256]{3,2,1,0:T(8,128)(2,1)}), bf16[64,2,64,256]{3,2,1,0:T(8,128)(2,1)}, u32[]{:S(2)}, u32[]{:S(2)}) %all-to-all-start) | async-done | bytes 4194336 | tf_op jit(solution)/shard_map/all_to_all | solution.py:324
  116.3 1.6 copy-done.12
  117.9 1.2 copy-done.14
  119.1 1.2 copy-done.16
  120.3 12.7 %outer_transforms.1 = (bf16[64,2,64,256]{3,2,1,0:T(8,128)(2,1)S(1)}, f32[296,128]{1,0:T(8,128)S(1)}) custom-call(bf16[64,2,64,256]{3,2,1,0:T(8,128)(2,1)} %all-to-all-done.r_hbm, bf16[512,512]{1,0:T(8,128)(2,1)S(1)} %copy-done.4, bf16[512,512]{1,0:T(8,128)(2,1)S(1)} %bitcast.13, bf16[512,512]{1,0:T(8,128)(2,1)S(1)} %copy-done.5, ...), custom_call_target="tpu_custom_call" | custom-call | flops 5368709120 | bytes 18874368 | tf_op jit(solution)/shard_map/outer_transforms/pallas_call | solution.py:351
  133.1 2.0 copy-done
  135.1 5.9 %all-to-all-start.1 = ((bf16[64,2,64,256]{3,2,1,0:T(8,128)(2,1)}), bf16[64,2,64,256]{3,2,1,0:T(8,128)(2,1)}, u32[]{:S(2)}, u32[]{:S(2)}) async-start(bf16[64,2,64,256]{3,2,1,0:T(8,128)(2,1)} %copy-done), calls=%async_computation.1 | async-start | bytes 8388608 | tf_op jit(solution)/shard_map/all_to_all | solution.py:365
  141.0 1.3 collective-permute-start
  142.4 1.8 collective-permute-done
  144.2 2.8 %collective-permute-start.1 = (f32[40,128]{1,0:T(8,128)S(1)}, f32[40,128]{1,0:T(8,128)S(1)}, u32[]{:S(2)}, u32[]{:S(2)}) collective-permute-start(f32[40,128]{1,0:T(8,128)S(1)} %slice_add_fusion), channel_id=1, source_target_pairs={{0,2},{1,3},{2,0},{3,1},{4,6},{5,7},{6,4},{7,5},{8,10},{9,11},{10,... | collective-permute-start | bytes 61448 | tf_op jit(solution)/shard_map/ppermute | solution.py:272
  146.9 1.8 collective-permute-done.1
  148.7 2.1 collective-permute-start.2
  150.8 1.0 collective-permute-done.2
  151.9 1.3 collective-permute-start.3
  153.2 8.5 %collective-permute-done.3 = f32[296,128]{1,0:T(8,128)S(1)} collective-permute-done((f32[296,128]{1,0:T(8,128)S(1)}, f32[296,128]{1,0:T(8,128)S(1)}, u32[]{:S(2)}, u32[]{:S(2)}) %collective-permute-start.3) | collective-permute-done | bytes 151584 | tf_op jit(solution)/shard_map/ppermute | solution.py:272
  161.7 2.9 %collective-permute-start.4 = (f32[296,128]{1,0:T(8,128)S(1)}, f32[296,128]{1,0:T(8,128)S(1)}, u32[]{:S(2)}, u32[]{:S(2)}) collective-permute-start(f32[296,128]{1,0:T(8,128)S(1)} %add.18), channel_id=1, source_target_pairs={{0,128},{4,132},{8,136},{12,140},{16,144},{20,148},{24,152},{28,15... | collective-permute-start | bytes 454664 | tf_op jit(solution)/shard_map/ppermute | solution.py:272
  164.6 5.4 %collective-permute-done.4 = f32[296,128]{1,0:T(8,128)S(1)} collective-permute-done((f32[296,128]{1,0:T(8,128)S(1)}, f32[296,128]{1,0:T(8,128)S(1)}, u32[]{:S(2)}, u32[]{:S(2)}) %collective-permute-start.4) | collective-permute-done | bytes 151584 | tf_op jit(solution)/shard_map/ppermute | solution.py:272
  170.0 0.0 copy-start.2
  170.0 0.0 copy-start.3
  170.0 1.7 collective-permute-start.5
  171.7 64.4 %collective-permute-done.5.other_ref = f32[296,128]{1,0:T(8,128)S(1)} collective-permute-done((f32[296,128]{1,0:T(8,128)S(1)}, f32[296,128]{1,0:T(8,128)S(1)}, u32[]{:S(2)}, u32[]{:S(2)}) %collective-permute-start.5) | collective-permute-done | bytes 151584 | tf_op jit(solution)/shard_map/ppermute | solution.py:272
  236.1 1.2 all-to-all-done.1.x_hbm.after_ref
  237.3 1.7 pair_sum.1.v_ref
  238.9 2.0 collective-permute-start.8
  240.9 2.7 %collective-permute-start.7 = (f32[296,128]{1,0:T(8,128)}, f32[296,128]{1,0:T(8,128)S(1)}, u32[]{:S(2)}, u32[]{:S(2)}) collective-permute-start(f32[296,128]{1,0:T(8,128)} %pair_sum.1.v_ref), channel_id=1, source_target_pairs={{0,32},{4,36},{8,40},{12,44},{16,48},{20,52},{24,56},{28,60},{32,0... | collective-permute-start | bytes 454664 | tf_op jit(solution)/shard_map/ppermute | solution.py:272
  243.7 0.9 collective-permute-start.6
  244.6 5.5 %token_gradients.1 = (bf16[8,512,256]{2,1,0:T(8,128)(2,1)}, bf16[8,512,256]{2,1,0:T(8,128)(2,1)}) custom-call(bf16[64,2,64,256]{3,2,1,0:T(8,128)(2,1)} %all-to-all-done.1.x_hbm.after_ref, bf16[8,512,256]{2,1,0:T(8,128)(2,1)S(1)} %bitcast.12, bf16[512,512]{1,0:T(8,128)(2,1)S(1)} %copy-done.3, bf16[512,512]{1,0:T(8,128)(2,1)S(1)} %copy-done.2), custom_call_target="tpu_custom_call" | custom-call | flops 2147483648 | bytes 10485760 | tf_op jit(solution)/shard_map/token_gradients/pallas_call | solution.py:379
  250.1 3.6 %collective-permute-done.8.c_ref = f32[296,128]{1,0:T(8,128)S(1)} collective-permute-done((f32[296,128]{1,0:T(8,128)}, f32[296,128]{1,0:T(8,128)S(1)}, u32[]{:S(2)}, u32[]{:S(2)}) %collective-permute-start.8) | collective-permute-done | bytes 151584 | tf_op jit(solution)/shard_map/ppermute | solution.py:272
  253.7 5.2 %collective-permute-done.6.a_ref = f32[296,128]{1,0:T(8,128)} collective-permute-done((f32[296,128]{1,0:T(8,128)}, f32[296,128]{1,0:T(8,128)}, u32[]{:S(2)}, u32[]{:S(2)}) %collective-permute-start.6) | collective-permute-done | bytes 151584 | tf_op jit(solution)/shard_map/ppermute | solution.py:272
  258.9 1.8 weight_gradients.1
  (39 shorter events, 0.2 us)
Async XLA Ops:
  6.8 13.6 %copy-start.6 = (bf16[128,256]{1,0:T(8,128)(2,1)S(1)}, bf16[128,256]{1,0:T(8,128)(2,1)}, u32[]{:S(2)}) copy-start(bf16[128,256]{1,0:T(8,128)(2,1)} %w_ref.1) | copy-start | bytes 196612
  6.9 13.7 %copy-start.21 = (f32[512,8]{0,1:T(8,128)S(1)}, f32[512,8]{0,1:T(8,128)}, u32[]{:S(2)}) copy-start(f32[512,8]{0,1:T(8,128)} %param.21) | copy-start | bytes 49156
  6.9 13.8 %copy-start.22 = (f32[512,8]{0,1:T(8,128)S(1)}, f32[512,8]{0,1:T(8,128)}, u32[]{:S(2)}) copy-start(f32[512,8]{0,1:T(8,128)} %param.22) | copy-start | bytes 49156
  6.9 14.0 %copy-start.4 = (bf16[512,512]{1,0:T(8,128)(2,1)S(1)}, bf16[512,512]{1,0:T(8,128)(2,1)}, u32[]{:S(2)}) copy-start(bf16[512,512]{1,0:T(8,128)(2,1)} %fo_ref.1) | copy-start | bytes 1572868
  6.9 14.2 %copy-start.5 = (bf16[512,512]{1,0:T(8,128)(2,1)S(1)}, bf16[512,512]{1,0:T(8,128)(2,1)}, u32[]{:S(2)}) copy-start(bf16[512,512]{1,0:T(8,128)(2,1)} %io_ref.1) | copy-start | bytes 1572868
  6.9 109.4 %all-to-all-start = ((bf16[64,2,64,256]{3,2,1,0:T(8,128)(2,1)}), bf16[64,2,64,256]{3,2,1,0:T(8,128)(2,1)}, u32[]{:S(2)}, u32[]{:S(2)}) async-start(bf16[64,2,64,256]{3,2,1,0:T(8,128)(2,1)} %inner_transforms.1), calls=%async_computation | async-start | bytes 8388608 | tf_op jit(solution)/shard_map/all_to_all | solution.py:324
  20.4 0.9 copy-start.7
  20.4 0.9 copy-start.8
  20.4 1.0 copy-start.9
  21.3 95.0 %copy-start.10 = (bf16[80,512]{1,0:T(8,128)(2,1)S(1)}, bf16[80,512]{1,0:T(8,128)(2,1)}, u32[]{:S(2)}) copy-start(bf16[80,512]{1,0:T(8,128)(2,1)} %constant.14.clone.tabt_ref) | copy-start | bytes 245764
  32.2 1.3 copy-start.11
  33.6 1.0 copy-start.13
  34.5 1.0 copy-start.15
  116.3 1.6 copy-start.12
  117.9 1.2 copy-start.14
  119.1 1.2 copy-start.16
  133.0 2.0 copy-start
  135.1 102.2 %all-to-all-start.1 = ((bf16[64,2,64,256]{3,2,1,0:T(8,128)(2,1)}), bf16[64,2,64,256]{3,2,1,0:T(8,128)(2,1)}, u32[]{:S(2)}, u32[]{:S(2)}) async-start(bf16[64,2,64,256]{3,2,1,0:T(8,128)(2,1)} %copy-done), calls=%async_computation.1 | async-start | bytes 8388608 | tf_op jit(solution)/shard_map/all_to_all | solution.py:365
  141.0 3.1 %collective-permute-start = (f32[40,128]{1,0:T(8,128)S(1)}, f32[40,128]{1,0:T(8,128)S(1)}, u32[]{:S(2)}, u32[]{:S(2)}) collective-permute-start(f32[40,128]{1,0:T(8,128)S(1)} %slice.7), channel_id=1, source_target_pairs={{0,1},{1,0},{2,3},{3,2},{4,5},{5,4},{6,7},{7,6},{8,9},{9,8},{10,11... | collective-permute-start | bytes 61448 | tf_op jit(solution)/shard_map/ppermute | solution.py:272
  144.2 4.5 %collective-permute-start.1 = (f32[40,128]{1,0:T(8,128)S(1)}, f32[40,128]{1,0:T(8,128)S(1)}, u32[]{:S(2)}, u32[]{:S(2)}) collective-permute-start(f32[40,128]{1,0:T(8,128)S(1)} %slice_add_fusion), channel_id=1, source_target_pairs={{0,2},{1,3},{2,0},{3,1},{4,6},{5,7},{6,4},{7,5},{8,10},{9,11},{10,... | collective-permute-start | bytes 61448 | tf_op jit(solution)/shard_map/ppermute | solution.py:272
  148.7 3.1 %collective-permute-start.2 = (f32[296,128]{1,0:T(8,128)S(1)}, f32[296,128]{1,0:T(8,128)S(1)}, u32[]{:S(2)}, u32[]{:S(2)}) collective-permute-start(f32[296,128]{1,0:T(8,128)S(1)} %pad_maximum_fusion), channel_id=1, source_target_pairs={{0,4},{4,0},{8,12},{12,8},{16,20},{20,16},{24,28},{28,24},{32,36},... | collective-permute-start | bytes 454664 | tf_op jit(solution)/shard_map/ppermute | solution.py:272
  151.9 9.8 %collective-permute-start.3 = (f32[296,128]{1,0:T(8,128)S(1)}, f32[296,128]{1,0:T(8,128)S(1)}, u32[]{:S(2)}, u32[]{:S(2)}) collective-permute-start(f32[296,128]{1,0:T(8,128)S(1)} %fusion), channel_id=1, source_target_pairs={{0,64},{4,68},{8,72},{12,76},{16,80},{20,84},{24,88},{28,92},{32,9... | collective-permute-start | bytes 454664 | tf_op jit(solution)/shard_map/ppermute | solution.py:272
  161.7 8.3 %collective-permute-start.4 = (f32[296,128]{1,0:T(8,128)S(1)}, f32[296,128]{1,0:T(8,128)S(1)}, u32[]{:S(2)}, u32[]{:S(2)}) collective-permute-start(f32[296,128]{1,0:T(8,128)S(1)} %add.18), channel_id=1, source_target_pairs={{0,128},{4,132},{8,136},{12,140},{16,144},{20,148},{24,152},{28,15... | collective-permute-start | bytes 454664 | tf_op jit(solution)/shard_map/ppermute | solution.py:272
  170.0 67.3 %copy-start.17 = (f32[296,128]{1,0:T(8,128)}, f32[296,128]{1,0:T(8,128)S(1)}, u32[]{:S(2)}) copy-start(f32[296,128]{1,0:T(8,128)S(1)} %add.19.one_ref) | copy-start | bytes 454660
  170.0 74.6 %copy-start.1 = (bf16[4096,256]{1,0:T(8,128)(2,1)S(1)}, bf16[4096,256]{1,0:T(8,128)(2,1)}, u32[]{:S(2)}) copy-start(bf16[4096,256]{1,0:T(8,128)(2,1)} %param.16) | copy-start | bytes 6291460
  170.0 74.6 %copy-start.2 = (bf16[512,512]{1,0:T(8,128)(2,1)S(1)}, bf16[512,512]{1,0:T(8,128)(2,1)}, u32[]{:S(2)}) copy-start(bf16[512,512]{1,0:T(8,128)(2,1)} %fi_ref.1) | copy-start | bytes 1572868
  170.0 74.6 %copy-start.3 = (bf16[512,512]{1,0:T(8,128)(2,1)S(1)}, bf16[512,512]{1,0:T(8,128)(2,1)}, u32[]{:S(2)}) copy-start(bf16[512,512]{1,0:T(8,128)(2,1)} %ii_ref.1) | copy-start | bytes 1572868
  170.0 66.0 %collective-permute-start.5 = (f32[296,128]{1,0:T(8,128)S(1)}, f32[296,128]{1,0:T(8,128)S(1)}, u32[]{:S(2)}, u32[]{:S(2)}) collective-permute-start(f32[296,128]{1,0:T(8,128)S(1)} %add.19.one_ref), channel_id=1, source_target_pairs={{0,8},{4,12},{8,0},{12,4},{16,24},{20,28},{24,16},{28,20},{32,40},... | collective-permute-start | bytes 454664 | tf_op jit(solution)/shard_map/ppermute | solution.py:272
  236.1 1.2 copy-start.20
  238.9 14.8 %collective-permute-start.8 = (f32[296,128]{1,0:T(8,128)}, f32[296,128]{1,0:T(8,128)S(1)}, u32[]{:S(2)}, u32[]{:S(2)}) collective-permute-start(f32[296,128]{1,0:T(8,128)} %pair_sum.1.v_ref), channel_id=1, source_target_pairs={{0,48},{4,52},{8,56},{12,60},{16,32},{20,36},{24,40},{28,44},{32,1... | collective-permute-start | bytes 454664 | tf_op jit(solution)/shard_map/ppermute | solution.py:272
  240.9 12.8 %collective-permute-start.7 = (f32[296,128]{1,0:T(8,128)}, f32[296,128]{1,0:T(8,128)S(1)}, u32[]{:S(2)}, u32[]{:S(2)}) collective-permute-start(f32[296,128]{1,0:T(8,128)} %pair_sum.1.v_ref), channel_id=1, source_target_pairs={{0,32},{4,36},{8,40},{12,44},{16,48},{20,52},{24,56},{28,60},{32,0... | collective-permute-start | bytes 454664 | tf_op jit(solution)/shard_map/ppermute | solution.py:272
  243.7 15.2 %collective-permute-start.6 = (f32[296,128]{1,0:T(8,128)}, f32[296,128]{1,0:T(8,128)}, u32[]{:S(2)}, u32[]{:S(2)}) collective-permute-start(f32[296,128]{1,0:T(8,128)} %pair_sum.1.v_ref), channel_id=1, source_target_pairs={{0,16},{4,20},{8,24},{12,28},{16,0},{20,4},{24,8},{28,12},{32,48},... | collective-permute-start | bytes 454664 | tf_op jit(solution)/shard_map/ppermute | solution.py:272
  253.7 5.2 %copy-start.18 = (f32[296,128]{1,0:T(8,128)}, f32[296,128]{1,0:T(8,128)S(1)}, u32[]{:S(2)}) copy-start(f32[296,128]{1,0:T(8,128)S(1)} %collective-permute-done.8.c_ref) | copy-start | bytes 454660
  253.7 5.2 %copy-start.19 = (f32[296,128]{1,0:T(8,128)}, f32[296,128]{1,0:T(8,128)S(1)}, u32[]{:S(2)}) copy-start(f32[296,128]{1,0:T(8,128)S(1)} %collective-permute-done.7.b_ref) | copy-start | bytes 454660

commit v2 on v1

--- a/solution.py
+++ b/solution.py
@@ -14,9 +14,10 @@
 MIB = 1 << 20
 PARTS = 64
 ROWS = 8
-OUTER_LIMIT = 40
+OUTER_LIMIT = 62
 CHUNKS = 4
-TABLE = 40
+PITCH = 520
+TABLE = 48
 
 
 def dot(x, y, precision=None):
@@ -118,11 +119,10 @@
     cos_ref[0] = jnp.cos(preact)
 
 
-def outer_kernel(
-    r_hbm, fo_ref, fot_ref, io_ref, iot_ref, w_ref, wt_ref, tabt_ref, tf_ref, ti_ref,
-    hid_hbm, hidt_hbm, cos_hbm, q_ref,
-    o_hbm, s_ref, x_ref, y_ref, wire_ref, hid_ref, hidt_ref, cos_ref, in_sem, gen_sem, out_sem,
-):
+def outer_kernel(r_hbm, *refs):
+    sources, (o_hbm, s_ref, x_ref, y_ref, out_ref, wire_ref, spec_ref), refs = refs[:13], refs[13:20], refs[20:]
+    targets, (in_sem, side_sem, out_sem) = refs[:13], refs[13:]
+    (fo_ref, tf_ref, w_ref, hid_ref, io_ref, ti_ref, iot_ref, fot_ref, hidt_ref, wt_ref, cos_ref, tabt_ref, q_ref) = targets
     size = fo_ref.shape[0]
     hidden, channels = w_ref.shape
     lanes = x_ref.shape[2]
@@ -140,46 +140,65 @@
         return copies
 
     loads = moved(r_hbm, wire_ref, in_sem)
-    for load in loads:
-        load.start()
-    generated = [
-        pltpu.make_async_copy(source, target, gen_sem.at[i])
-        for i, (source, target) in enumerate(((hid_hbm, hid_ref), (hidt_hbm, hidt_ref), (cos_hbm, cos_ref)))
-    ]
-    for copy in generated:
+    aside = [pltpu.make_async_copy(source, target, side_sem.at[i]) for i, (source, target) in enumerate(zip(sources, targets))]
+    for copy in aside[:2] + loads[:CHUNKS] + aside[2:6] + loads[CHUNKS:] + aside[6:]:
         copy.start()
-
-    for which, ref in ((0, x_ref), (1, y_ref)):
+    sends = moved(wire_ref, o_hbm, out_sem)
+
+    def spread(which, ref):
         for c in range(CHUNKS):
             loads[which * CHUNKS + c].wait()
             for part in range(c * chunk, (c + 1) * chunk):
                 for i in range(split):
                     ref[i, part * rows : (part + 1) * rows] = wire_ref[part, which, :, i * lanes : (i + 1) * lanes].astype(F32)
-    for copy in generated:
+
+    def send(which):
+        for c in range(CHUNKS):
+            for part in range(c * chunk, (c + 1) * chunk):
+                for i in range(split):
+                    lane = slice(i * lanes, (i + 1) * lanes)
+                    value = [out_ref[i, pl.ds(part * ROWS + a, ROWS, stride=PITCH), :] for a in range(ROWS)]
+                    wire_ref[part, which, :, lane] = jnp.concatenate(value, 0).astype(BF16)
+            sends[which * CHUNKS + c].start()
+
+    def load(ref, k, scale_ref):
+        scale = jnp.broadcast_to(scale_ref[:, k : k + 1], (size, lanes))
+        mine = pl.ds(k, size, stride=ROWS)
+        return jnp.concatenate([(scale * ref[i, mine, :]).astype(BF16) for i in range(split)], 1)
+
+    def store(k, scale_ref, value):
+        scale = jnp.broadcast_to(scale_ref[:, k : k + 1], (size, lanes))
+        for i in range(split):
+            out_ref[i, k * PITCH : k * PITCH + size] = scale * value[:, i * lanes : (i + 1) * lanes]
+
+    spread(0, x_ref)
+    for copy in aside[:6]:
+        copy.wait()
+    coming = dot(fo_ref[...], load(x_ref, 0, tf_ref)).astype(BF16)
+    for k in range(ROWS):
+        spectrum = coming
+        spec_ref[k] = spectrum
+        if k + 1 < ROWS:
+            coming = dot(fo_ref[...], load(x_ref, k + 1, tf_ref)).astype(BF16)
+        filtered = (dot(hid_ref[k], w_ref[...]) * spectrum.astype(F32)).astype(BF16)
+        store(k, ti_ref, dot(io_ref[...], filtered))
+    spread(1, y_ref)
+    send(0)
+    for copy in aside[6:]:
         copy.wait()
 
     weight = jnp.zeros((hidden, channels), F32)
     layer = [jnp.zeros((halves, hidden), F32)] * 2
     bias = jnp.zeros((TABLE - 2 * halves, hidden), F32)
     pending = []
+    coming = dot(iot_ref[...], load(y_ref, 0, ti_ref))
     for k in range(ROWS):
-        mine = pl.ds(k, size, stride=ROWS)
-        tf = jnp.broadcast_to(tf_ref[:, k : k + 1], (size, lanes))
-        ti = jnp.broadcast_to(ti_ref[:, k : k + 1], (size, lanes))
-
-        def load(ref, scale):
-            return jnp.concatenate([(scale * ref[i, mine, :]).astype(BF16) for i in range(split)], 1)
-
-        def store(ref, scale, value):
-            for i in range(split):
-                ref[i, mine, :] = scale * value[:, i * lanes : (i + 1) * lanes]
-
-        spectrum = dot(fo_ref[...], load(x_ref, tf)).astype(BF16).astype(F32)
-        grad_filtered = dot(iot_ref[...], load(y_ref, ti))
+        grad_filtered = coming
+        if k + 1 < ROWS:
+            coming = dot(iot_ref[...], load(y_ref, k + 1, ti_ref))
         kernel = dot(hid_ref[k], w_ref[...])
-        store(x_ref, ti, dot(io_ref[...], (kernel * spectrum).astype(BF16)))
-        store(y_ref, tf, dot(fot_ref[...], (grad_filtered * kernel).astype(BF16)))
-        grad_kernel = (grad_filtered * spectrum).astype(BF16)
+        store(k, tf_ref, dot(fot_ref[...], (grad_filtered * kernel).astype(BF16)))
+        grad_kernel = (grad_filtered * spec_ref[k].astype(F32)).astype(BF16)
         weight = weight + dot(hidt_ref[k], grad_kernel)
         pending.append(dot(grad_kernel, wt_ref[...]) * cos_ref[k])
         if len(pending) == 2:
@@ -195,21 +214,14 @@
                 ms, mc = part[:halves], part[halves : 2 * halves]
                 layer = [layer[0] + cq * ms + sq * mc, layer[1] + cq * mc - sq * ms]
                 bias = bias + part[2 * halves :]
-
-    sends = moved(wire_ref, o_hbm, out_sem)
-    for which, ref in ((0, x_ref), (1, y_ref)):
-        for c in range(CHUNKS):
-            for part in range(c * chunk, (c + 1) * chunk):
-                for i in range(split):
-                    wire_ref[part, which, :, i * lanes : (i + 1) * lanes] = ref[i, part * rows : (part + 1) * rows].astype(BF16)
-            sends[which * CHUNKS + c].start()
+    send(1)
 
     scale = 1.0 / size
     for i in range(split):
         s_ref[i * hidden : (i + 1) * hidden] = weight[:, i * lanes : (i + 1) * lanes] * scale
     s_ref[split * hidden :] = jnp.concatenate(layer + [bias], 0) * scale
-    for send in sends:
-        send.wait()
+    for copy in sends:
+        copy.wait()
 
 
 def tokens_kernel(x_hbm, dy_ref, ii_ref, fi_ref, gi_hbm, gg_hbm, x_ref, gi_ref, gg_ref, in_sem, out_sem):
@@ -246,20 +258,22 @@
         send.wait()
 
 
-def pair_kernel(one_ref, other_ref, after_ref, o_ref):
-    o_ref[...] = one_ref[...] + other_ref[...]
-
-
-def finish_kernel(v_ref, a_ref, b_ref, c_ref, after_ref, w_ref, l_ref, b_out_ref):
-    hidden, channels = w_ref.shape
+def finish_kernel(core_ref, mine_ref, other_ref, w_ref, l_ref, b_ref):
+    hidden = w_ref.shape[0]
     features = l_ref.shape[0]
-    lanes = v_ref.shape[1]
-    total = (v_ref[...] + a_ref[...]) + (b_ref[...] + c_ref[...])
-    split = channels // lanes
-    for i in range(split):
-        w_ref[:, i * lanes : (i + 1) * lanes] = total[i * hidden : (i + 1) * hidden]
-    l_ref[...] = total[split * hidden : split * hidden + features]
-    b_out_ref[...] = total[split * hidden + features : split * hidden + features + 1]
+    half, lanes = mine_ref.shape
+    mine, other = mine_ref[...], other_ref[...]
+    lower = jnp.where(core_ref[0] == 0, mine, other)
+    upper = jnp.where(core_ref[0] == 0, other, mine)
+    w_ref[:, :lanes] = lower[:hidden]
+    w_ref[: half - hidden, lanes:] = lower[hidden:]
+    w_ref[half - hidden :, lanes:] = upper[: 2 * hidden - half]
+    l_ref[...] = upper[2 * hidden - half : 2 * hidden - half + features]
+    b_ref[...] = upper[2 * hidden - half + features : 2 * hidden - half + features + 1]
+
+
+def after(value, *others):
+    return lax.optimization_barrier((value,) + others)[0]
 
 
 def params(limit, axes=1):
@@ -348,33 +362,37 @@
     small = (2 * hidden + TABLE, lanes)
     high = table.T.astype(BF16)
     low = (table.T - high.astype(np.float32)).astype(BF16)
+    hid, hidt, cosine, turns = generated
+    aside = [
+        forward_outer, twiddle_forward, filter_out, hid, inverse_outer, twiddle_inverse,
+        inverse_outer.T, forward_outer.T, hidt, filter_out.T, cosine, np.concatenate([high, low], 0), turns,
+    ]
     returned, partial = pl.pallas_call(
         outer_kernel,
         out_shape=[jax.ShapeDtypeStruct(wire, BF16), jax.ShapeDtypeStruct(small, F32)],
-        in_specs=[anywhere] + [inside] * 9 + [anywhere] * 3 + [inside],
+        in_specs=[anywhere] * 14,
         out_specs=[anywhere, inside],
         scratch_shapes=[pltpu.VMEM((channels // lanes, ROWS * size, lanes), F32)] * 2
-        + [pltpu.VMEM(wire, BF16)]
-        + [pltpu.VMEM((ROWS,) + shape, kind) for shape, kind in made[:3]]
-        + [pltpu.SemaphoreType.DMA((count,)) for count in (2 * CHUNKS, 3, 2 * CHUNKS)],
+        + [pltpu.VMEM((channels // lanes, ROWS * PITCH, lanes), F32)]
+        + [pltpu.VMEM(wire, BF16), pltpu.VMEM(tokens, BF16)]
+        + [pltpu.VMEM(array.shape, array.dtype) for array in aside]
+        + [pltpu.SemaphoreType.DMA((count,)) for count in (2 * CHUNKS, len(aside), 2 * CHUNKS)],
         compiler_params=pltpu.CompilerParams(vmem_limit_bytes=OUTER_LIMIT * MIB),
         cost_estimate=pl.CostEstimate(flops=10 * ROWS * size * size * channels, bytes_accessed=18 * MIB, transcendentals=0),
         name="outer_transforms",
-    )(received, forward_outer, forward_outer.T, inverse_outer, inverse_outer.T, filter_out, filter_out.T, np.concatenate([high, low], 0), twiddle_forward, twiddle_inverse, *generated)
+    )(received, *aside)
 
     arrived = lax.all_to_all(returned, "seq", split_axis=0, concat_axis=0, tiled=True)
 
     layer = doubled(partial[2 * hidden :], "ch", 4, (1, 2))
     total = jnp.concatenate([partial[: 2 * hidden], layer], 0)
-    total = doubled(total, "seq", PARTS, (1, 16, 32))
-    total = pl.pallas_call(
-        pair_kernel,
-        out_shape=jax.ShapeDtypeStruct(small, F32),
-        in_specs=[inside, inside, anywhere],
-        out_specs=inside,
-        name="pair_sum",
-    )(total, exchanged(total, "seq", PARTS, 2), arrived)
-    others = [exchanged(total, "seq", PARTS, step) for step in (4, 8, 12)]
+    half = small[0] // 2
+    lower, upper = total[:half], total[half:]
+    core = lax.axis_index("seq") % 2
+    mine = jnp.where(core == 0, lower, upper)
+    mine = mine + exchanged(jnp.where(core == 0, upper, lower), "seq", PARTS, 1)
+    mine = doubled(mine, "seq", PARTS, (16, 32, 8))
+    other = exchanged(mine, "seq", PARTS, 4)
 
     grad_input, grad_gate = pl.pallas_call(
         tokens_kernel,
@@ -386,6 +404,7 @@
         cost_estimate=pl.CostEstimate(flops=4 * ROWS * size * size * channels, bytes_accessed=10 * MIB, transcendentals=0),
         name="token_gradients",
     )(arrived, upstream, inverse_inner, forward_inner)
+    mine = doubled(mine + after(other, grad_gate), "seq", PARTS, (2,))
     weight_grad, layer_grad, bias_grad = pl.pallas_call(
         finish_kernel,
         out_shape=[
@@ -393,9 +412,9 @@
             jax.ShapeDtypeStruct((features, hidden), F32),
             jax.ShapeDtypeStruct((1, hidden), F32),
         ],
-        in_specs=[inside] * 4 + [anywhere],
+        in_specs=[pl.BlockSpec(memory_space=pltpu.SMEM), inside, inside],
         name="weight_gradients",
-    )(total, *others, grad_gate)
+    )(core.astype(jnp.int32).reshape(1), mine, exchanged(mine, "seq", PARTS, 1))
     flat = (ROWS * size, channels)
     return grad_input.reshape(flat), grad_gate.reshape(flat), weight_grad, layer_grad, bias_grad.reshape(hidden)
 

time: 261 us -> 252 us (0.966)
  waiting for transfers between devices: 174 us -> 162 us
    ppermute x9, waiting for transfers between devices: 91.6 us -> 85.9 us  [exchanged(): return lax.ppermute(value, axis, [(i, i ^ step) for i in range(count)])]
    all_to_all x1, waiting for transfers between devices: 80.7 us -> 76.3 us  [shards(): lax.all_to_all(sent, 'seq', split_axis=0, concat_axis=0, tiled=True)]
    pallas_call x1, Pallas kernels: 12.7 us -> 16 us  [shards(): pl.pallas_call(outer_kernel, out_shape=[jax.ShapeDtypeStruct(wire, BF16),...]
    unnamed x51 -> x41, local copies, waits for them, and re-layouts: 10.3 us -> 9.1 us
  transfers between devices with their start and end apart: 11 -> 11, of which waited for: 10 -> 9; matrix products, arithmetic and copies ran while one was open for 0% -> 2% of each run, Pallas kernels for 6% -> 7%
where the time goes in v2:
time: 252 us
  waiting for transfers between devices  162 us (64%)
  Pallas kernels  40.2 us (16%)
  starting transfers between devices  39.6 us (16%)
  local copies, waits for them, and re-layouts  9.11 us (4%)
    ppermute x9, waiting for transfers between devices, exchanged(): return lax.ppermute(value, axis, [(i, i ^ step) for i in range(count)])  85.9 us
    all_to_all x1, waiting for transfers between devices, shards(): lax.all_to_all(sent, 'seq', split_axis=0, concat_axis=0, tiled=True)  76.3 us
    ppermute x9, starting transfers between devices, exchanged(): return lax.ppermute(value, axis, [(i, i ^ step) for i in range(count)])  19.9 us
    pallas_call x1, Pallas kernels, shards(): pl.pallas_call(outer_kernel, out_shape=[jax.ShapeDtypeStruct(wire, BF16),...  16 us
    all_to_all x1, starting transfers between devices, shards(): lax.all_to_all(sent, 'seq', split_axis=0, concat_axis=0, tiled=True)  13.5 us
    pallas_call x1, Pallas kernels, shards(): pl.pallas_call(filter_kernel, grid_spec=pltpu.PrefetchScalarGridSpec(num_...  11 us
    unnamed x41, local copies, waits for them, and re-layouts  9.1 us
    all_to_all x1, starting transfers between devices, shards(): lax.all_to_all(returned, 'seq', split_axis=0, concat_axis=0, tiled=True)  6.21 us
  transfers between devices with their start and end apart: 11, of which 9 were waited for; matrix products, arithmetic and copies ran while one was open for 2% of the time, Pallas kernels for 7%

profile of v2, /device:TPU:1, one launch (start us, length us, event | category | flops | bytes accessed | tf_op | source)
XLA Modules:
  0.0 252.2 jit_solution(4290145163512378726)
XLA Ops:
  0.6 6.1 %inner_transforms.1 = bf16[64,2,64,256]{3,2,1,0:T(8,128)(2,1)} custom-call(bf16[8,512,256]{2,1,0:T(8,128)(2,1)} %bitcast.15, bf16[8,512,256]{2,1,0:T(8,128)(2,1)} %bitcast.16, bf16[8,512,256]{2,1,0:T(8,128)(2,1)} %bitcast.12, bf16[512,512]{1,0:T(8,128)(2,1)} %fi_ref.1, bf16[512,512]{1,0:T(8,128)(2,1)} %ii_ref.1), custom_call_target="tpu_custom_call" | custom-call | flops 2147483648 | bytes 10485760 | tf_op jit(solution)/shard_map/inner_transforms/pallas_call | solution.py:323
  6.7 0.0 copy-start.12
  6.7 0.0 copy-start.11
  6.8 13.5 %all-to-all-start = ((bf16[64,2,64,256]{3,2,1,0:T(8,128)(2,1)}), bf16[64,2,64,256]{3,2,1,0:T(8,128)(2,1)}, u32[]{:S(2)}, u32[]{:S(2)}) async-start(bf16[64,2,64,256]{3,2,1,0:T(8,128)(2,1)} %inner_transforms.1), calls=%async_computation | async-start | bytes 8388608 | tf_op jit(solution)/shard_map/all_to_all | solution.py:338
  20.3 0.0 copy-start.16
  20.3 0.0 copy-start.17
  20.3 0.0 copy-start.15
  20.3 0.0 copy-start.3
  20.3 0.0 copy-start.4
  20.3 0.0 copy-start.5
  20.3 1.0 copy.19
  21.3 1.0 copy.20
  22.3 0.9 copy.22.refs_1_
  23.2 0.8 copy.23.refs_5_
  24.0 0.7 copy.21
  24.8 11.0 %filter_generator.1 = (bf16[8,512,128]{2,1,0:T(8,128)(2,1)S(1)}, bf16[8,128,512]{2,1,0:T(8,128)(2,1)S(1)}, f32[8,512,128]{2,1,0:T(8,128)S(1)}, f32[8,32,128]{2,1,0:T(8,128)S(1)}) custom-call(s32[1]{0:T(128)} %bitcast.3.col_ref, f32[512,48]{1,0:T(8,128)S(1)} %copy-done.5, f32[32,128]{1,0:T(8,128)S(1)} %copy-done.3, f32[1,128]{1,0:T(1,128)S(1)} %bitcast.14), custom_call_target="tpu_custom_call" | custom-call | flops 41943040 | bytes 9437184 | tf_op jit(solution)/shard_map/filter_generator/pallas_call | solution.py:348
  35.8 0.0 copy-start.6
  35.8 1.3 copy-done.6
  37.2 1.0 copy-done.7
  38.1 1.0 copy-done.8
  39.2 0.7 copy-done.9
  39.8 76.3 %all-to-all-done.r_hbm = bf16[64,2,64,256]{3,2,1,0:T(8,128)(2,1)} async-done(((bf16[64,2,64,256]{3,2,1,0:T(8,128)(2,1)}), bf16[64,2,64,256]{3,2,1,0:T(8,128)(2,1)}, u32[]{:S(2)}, u32[]{:S(2)}) %all-to-all-start) | async-done | bytes 4194336 | tf_op jit(solution)/shard_map/all_to_all | solution.py:338
  116.1 16.0 %outer_transforms.1 = (bf16[64,2,64,256]{3,2,1,0:T(8,128)(2,1)}, f32[304,128]{1,0:T(8,128)}) custom-call(bf16[64,2,64,256]{3,2,1,0:T(8,128)(2,1)} %all-to-all-done.r_hbm, bf16[512,512]{1,0:T(8,128)(2,1)} %refs_0_.1, f32[512,8]{1,0:T(8,128)} %copy.22.refs_1_, bf16[128,256]{1,0:T(8,128)(2,1)} %refs_2_.1, bf16[8,512,128]{2,1,0:T(8,128)(2,1)} %copy-done.7, ...), custom_call_target="tpu_custom_call" | custom-call | flops 5368709120 | bytes 18874368 | tf_op jit(solution)/shard_map/outer_transforms/pallas_call | solution.py:370
  132.1 0.0 copy-start
  132.1 0.0 copy-start.1
  132.1 0.0 copy-start.2
  132.1 6.2 %all-to-all-start.1 = ((bf16[64,2,64,256]{3,2,1,0:T(8,128)(2,1)}), bf16[64,2,64,256]{3,2,1,0:T(8,128)(2,1)}, u32[]{:S(2)}, u32[]{:S(2)}) async-start(bf16[64,2,64,256]{3,2,1,0:T(8,128)(2,1)} %get-tuple-element.25), calls=%async_computation.1 | async-start | bytes 8388608 | tf_op jit(solution)/shard_map/all_to_all | solution.py:385
  138.4 1.3 collective-permute-start
  139.7 1.9 collective-permute-done
  141.6 2.7 %collective-permute-start.1 = (f32[48,128]{1,0:T(8,128)S(1)}, f32[48,128]{1,0:T(8,128)S(1)}, u32[]{:S(2)}, u32[]{:S(2)}) collective-permute-start(f32[48,128]{1,0:T(8,128)S(1)} %slice_add_fusion), channel_id=1, source_target_pairs={{0,2},{1,3},{2,0},{3,1},{4,6},{5,7},{6,4},{7,5},{8,10},{9,11},{10,... | collective-permute-start | bytes 73736 | tf_op jit(solution)/shard_map/ppermute | solution.py:286
  144.3 1.8 collective-permute-done.1
  146.2 2.3 collective-permute-start.2
  148.5 0.9 collective-permute-done.2
  149.4 1.1 collective-permute-start.3
  150.5 5.9 %collective-permute-done.3 = f32[152,128]{1,0:T(8,128)S(1)} collective-permute-done((f32[152,128]{1,0:T(8,128)S(1)}, f32[152,128]{1,0:T(8,128)S(1)}, u32[]{:S(2)}, u32[]{:S(2)}) %collective-permute-start.3) | collective-permute-done | bytes 77856 | tf_op jit(solution)/shard_map/ppermute | solution.py:286
  156.4 2.7 %collective-permute-start.4 = (f32[152,128]{1,0:T(8,128)S(1)}, f32[152,128]{1,0:T(8,128)S(1)}, u32[]{:S(2)}, u32[]{:S(2)}) collective-permute-start(f32[152,128]{1,0:T(8,128)S(1)} %add.32), channel_id=1, source_target_pairs={{0,128},{4,132},{8,136},{12,140},{16,144},{20,148},{24,152},{28,15... | collective-permute-start | bytes 233480 | tf_op jit(solution)/shard_map/ppermute | solution.py:286
  159.1 4.7 %collective-permute-done.4 = f32[152,128]{1,0:T(8,128)S(1)} collective-permute-done((f32[152,128]{1,0:T(8,128)S(1)}, f32[152,128]{1,0:T(8,128)S(1)}, u32[]{:S(2)}, u32[]{:S(2)}) %collective-permute-start.4) | collective-permute-done | bytes 77856 | tf_op jit(solution)/shard_map/ppermute | solution.py:286
  163.8 3.7 %collective-permute-start.5 = (f32[152,128]{1,0:T(8,128)S(1)}, f32[152,128]{1,0:T(8,128)S(1)}, u32[]{:S(2)}, u32[]{:S(2)}) collective-permute-start(f32[152,128]{1,0:T(8,128)S(1)} %add.33), channel_id=1, source_target_pairs={{0,32},{4,36},{8,40},{12,44},{16,48},{20,52},{24,56},{28,60},{32,0... | collective-permute-start | bytes 233480 | tf_op jit(solution)/shard_map/ppermute | solution.py:286
  167.5 68.0 %collective-permute-done.5 = f32[152,128]{1,0:T(8,128)S(1)} collective-permute-done((f32[152,128]{1,0:T(8,128)S(1)}, f32[152,128]{1,0:T(8,128)S(1)}, u32[]{:S(2)}, u32[]{:S(2)}) %collective-permute-start.5) | collective-permute-done | bytes 77856 | tf_op jit(solution)/shard_map/ppermute | solution.py:286
  235.5 0.1 collective-permute-start.6
  235.6 0.0 all-to-all-done.1.x_hbm
  235.7 5.5 %token_gradients.1 = (bf16[8,512,256]{2,1,0:T(8,128)(2,1)}, bf16[8,512,256]{2,1,0:T(8,128)(2,1)}) custom-call(bf16[64,2,64,256]{3,2,1,0:T(8,128)(2,1)} %all-to-all-done.1.x_hbm, bf16[8,512,256]{2,1,0:T(8,128)(2,1)S(1)} %bitcast.13, bf16[512,512]{1,0:T(8,128)(2,1)S(1)} %copy-done.2, bf16[512,512]{1,0:T(8,128)(2,1)S(1)} %copy-done.1), custom_call_target="tpu_custom_call" | custom-call | flops 2147483648 | bytes 10485760 | tf_op jit(solution)/shard_map/token_gradients/pallas_call | solution.py:397
  241.2 2.5 %collective-permute-start.7 = (f32[152,128]{1,0:T(8,128)S(1)}, f32[152,128]{1,0:T(8,128)S(1)}, u32[]{:S(2)}, u32[]{:S(2)}) collective-permute-start(f32[152,128]{1,0:T(8,128)S(1)} %add.35), channel_id=1, source_target_pairs={{0,8},{4,12},{8,0},{12,4},{16,24},{20,28},{24,16},{28,20},{32,40},... | collective-permute-start | bytes 233480 | tf_op jit(solution)/shard_map/ppermute | solution.py:286
  243.8 1.8 collective-permute-done.7
  245.6 3.4 %collective-permute-start.8 = (f32[152,128]{1,0:T(8,128)S(1)}, f32[152,128]{1,0:T(8,128)S(1)}, u32[]{:S(2)}, u32[]{:S(2)}) collective-permute-start(f32[152,128]{1,0:T(8,128)S(1)} %add.36.mine_ref), channel_id=1, source_target_pairs={{0,4},{4,0},{8,12},{12,8},{16,20},{20,16},{24,28},{28,24},{32,36},... | collective-permute-start | bytes 233480 | tf_op jit(solution)/shard_map/ppermute | solution.py:286
  249.0 0.9 collective-permute-done.8.other_ref
  249.9 0.6 copy-done.14
  250.6 1.6 weight_gradients.1
  (31 shorter events, 0.2 us)
Async XLA Ops:
  6.7 13.5 %copy-start.12 = (bf16[512,512]{1,0:T(8,128)(2,1)S(1)}, bf16[512,512]{1,0:T(8,128)(2,1)}, u32[]{:S(2)}) copy-start(bf16[512,512]{1,0:T(8,128)(2,1)} %refs_4_.1) | copy-start | bytes 1572868
  6.7 14.6 %copy-start.11 = (bf16[512,512]{1,0:T(8,128)(2,1)S(1)}, bf16[512,512]{1,0:T(8,128)(2,1)}, u32[]{:S(2)}) copy-start(bf16[512,512]{1,0:T(8,128)(2,1)} %refs_0_.1) | copy-start | bytes 1572868
  6.8 109.4 %all-to-all-start = ((bf16[64,2,64,256]{3,2,1,0:T(8,128)(2,1)}), bf16[64,2,64,256]{3,2,1,0:T(8,128)(2,1)}, u32[]{:S(2)}, u32[]{:S(2)}) async-start(bf16[64,2,64,256]{3,2,1,0:T(8,128)(2,1)} %inner_transforms.1), calls=%async_computation | async-start | bytes 8388608 | tf_op jit(solution)/shard_map/all_to_all | solution.py:338
  20.3 2.1 copy-start.16
  20.3 2.9 %copy-start.17 = (f32[512,8]{0,1:T(8,128)S(1)}, f32[512,8]{0,1:T(8,128)}, u32[]{:S(2)}) copy-start(f32[512,8]{0,1:T(8,128)} %param.22) | copy-start | bytes 49156
  20.3 3.8 %copy-start.15 = (bf16[128,256]{1,0:T(8,128)(2,1)S(1)}, bf16[128,256]{1,0:T(8,128)(2,1)}, u32[]{:S(2)}) copy-start(bf16[128,256]{1,0:T(8,128)(2,1)} %refs_2_.1) | copy-start | bytes 196612
  20.3 4.5 %copy-start.3 = (f32[32,128]{1,0:T(8,128)S(1)}, f32[32,128]{1,0:T(8,128)}, u32[]{:S(2)}) copy-start(f32[32,128]{1,0:T(8,128)} %fin_ref.1) | copy-start | bytes 49156
  20.3 4.5 %copy-start.4 = (f32[128]{0:T(128)S(1)}, f32[128]{0:T(128)}, u32[]{:S(2)}) copy-start(f32[128]{0:T(128)} %param.24) | copy-start | bytes 1540
  20.3 4.5 %copy-start.5 = (f32[512,48]{1,0:T(8,128)S(1)}, f32[512,48]{1,0:T(8,128)}, u32[]{:S(2)}) copy-start(f32[512,48]{1,0:T(8,128)} %constant.27.clone.tab_ref) | copy-start | bytes 294916
  35.8 1.3 copy-start.6
  37.2 1.0 copy-start.7
  38.1 1.0 copy-start.8
  39.2 0.7 copy-start.9
  132.1 6.3 %copy-start.10 = (f32[304,128]{1,0:T(8,128)S(1)}, f32[304,128]{1,0:T(8,128)}, u32[]{:S(2)}) copy-start(f32[304,128]{1,0:T(8,128)} %get-tuple-element.28) | copy-start | bytes 466948
  132.1 103.5 %copy-start = (bf16[4096,256]{1,0:T(8,128)(2,1)S(1)}, bf16[4096,256]{1,0:T(8,128)(2,1)}, u32[]{:S(2)}) copy-start(bf16[4096,256]{1,0:T(8,128)(2,1)} %param.16) | copy-start | bytes 6291460
  132.1 103.5 %copy-start.1 = (bf16[512,512]{1,0:T(8,128)(2,1)S(1)}, bf16[512,512]{1,0:T(8,128)(2,1)}, u32[]{:S(2)}) copy-start(bf16[512,512]{1,0:T(8,128)(2,1)} %fi_ref.1) | copy-start | bytes 1572868
  132.1 103.5 %copy-start.2 = (bf16[512,512]{1,0:T(8,128)(2,1)S(1)}, bf16[512,512]{1,0:T(8,128)(2,1)}, u32[]{:S(2)}) copy-start(bf16[512,512]{1,0:T(8,128)(2,1)} %ii_ref.1) | copy-start | bytes 1572868
  132.1 103.5 %all-to-all-start.1 = ((bf16[64,2,64,256]{3,2,1,0:T(8,128)(2,1)}), bf16[64,2,64,256]{3,2,1,0:T(8,128)(2,1)}, u32[]{:S(2)}, u32[]{:S(2)}) async-start(bf16[64,2,64,256]{3,2,1,0:T(8,128)(2,1)} %get-tuple-element.25), calls=%async_computation.1 | async-start | bytes 8388608 | tf_op jit(solution)/shard_map/all_to_all | solution.py:385
  138.4 3.2 %collective-permute-start = (f32[48,128]{1,0:T(8,128)S(1)}, f32[48,128]{1,0:T(8,128)S(1)}, u32[]{:S(2)}, u32[]{:S(2)}) collective-permute-start(f32[48,128]{1,0:T(8,128)S(1)} %slice.15), channel_id=1, source_target_pairs={{0,1},{1,0},{2,3},{3,2},{4,5},{5,4},{6,7},{7,6},{8,9},{9,8},{10,11... | collective-permute-start | bytes 73736 | tf_op jit(solution)/shard_map/ppermute | solution.py:286
  141.6 4.6 %collective-permute-start.1 = (f32[48,128]{1,0:T(8,128)S(1)}, f32[48,128]{1,0:T(8,128)S(1)}, u32[]{:S(2)}, u32[]{:S(2)}) collective-permute-start(f32[48,128]{1,0:T(8,128)S(1)} %slice_add_fusion), channel_id=1, source_target_pairs={{0,2},{1,3},{2,0},{3,1},{4,6},{5,7},{6,4},{7,5},{8,10},{9,11},{10,... | collective-permute-start | bytes 73736 | tf_op jit(solution)/shard_map/ppermute | solution.py:286
  146.2 3.3 %collective-permute-start.2 = (f32[152,128]{1,0:T(8,128)S(1)}, f32[152,128]{1,0:T(8,128)S(1)}, u32[]{:S(2)}, u32[]{:S(2)}) collective-permute-start(f32[152,128]{1,0:T(8,128)S(1)} %slice_select_fusion), channel_id=1, source_target_pairs={{0,4},{4,0},{8,12},{12,8},{16,20},{20,16},{24,28},{28,24},{32,36},... | collective-permute-start | bytes 233480 | tf_op jit(solution)/shard_map/ppermute | solution.py:286
  149.4 6.9 %collective-permute-start.3 = (f32[152,128]{1,0:T(8,128)S(1)}, f32[152,128]{1,0:T(8,128)S(1)}, u32[]{:S(2)}, u32[]{:S(2)}) collective-permute-start(f32[152,128]{1,0:T(8,128)S(1)} %select_add_fusion), channel_id=1, source_target_pairs={{0,64},{4,68},{8,72},{12,76},{16,80},{20,84},{24,88},{28,92},{32,9... | collective-permute-start | bytes 233480 | tf_op jit(solution)/shard_map/ppermute | solution.py:286
  156.4 7.4 %collective-permute-start.4 = (f32[152,128]{1,0:T(8,128)S(1)}, f32[152,128]{1,0:T(8,128)S(1)}, u32[]{:S(2)}, u32[]{:S(2)}) collective-permute-start(f32[152,128]{1,0:T(8,128)S(1)} %add.32), channel_id=1, source_target_pairs={{0,128},{4,132},{8,136},{12,140},{16,144},{20,148},{24,152},{28,15... | collective-permute-start | bytes 233480 | tf_op jit(solution)/shard_map/ppermute | solution.py:286
  163.8 71.7 %collective-permute-start.5 = (f32[152,128]{1,0:T(8,128)S(1)}, f32[152,128]{1,0:T(8,128)S(1)}, u32[]{:S(2)}, u32[]{:S(2)}) collective-permute-start(f32[152,128]{1,0:T(8,128)S(1)} %add.33), channel_id=1, source_target_pairs={{0,32},{4,36},{8,40},{12,44},{16,48},{20,52},{24,56},{28,60},{32,0... | collective-permute-start | bytes 233480 | tf_op jit(solution)/shard_map/ppermute | solution.py:286
  235.5 5.7 %collective-permute-start.6 = (f32[152,128]{1,0:T(8,128)S(1)}, f32[152,128]{1,0:T(8,128)S(1)}, u32[]{:S(2)}, u32[]{:S(2)}) collective-permute-start(f32[152,128]{1,0:T(8,128)S(1)} %add.34), channel_id=1, source_target_pairs={{0,16},{4,20},{8,24},{12,28},{16,0},{20,4},{24,8},{28,12},{32,48},... | collective-permute-start | bytes 233480 | tf_op jit(solution)/shard_map/ppermute | solution.py:286
  241.2 4.3 %collective-permute-start.7 = (f32[152,128]{1,0:T(8,128)S(1)}, f32[152,128]{1,0:T(8,128)S(1)}, u32[]{:S(2)}, u32[]{:S(2)}) collective-permute-start(f32[152,128]{1,0:T(8,128)S(1)} %add.35), channel_id=1, source_target_pairs={{0,8},{4,12},{8,0},{12,4},{16,24},{20,28},{24,16},{28,20},{32,40},... | collective-permute-start | bytes 233480 | tf_op jit(solution)/shard_map/ppermute | solution.py:286
  245.6 4.4 %copy-start.13 = (f32[152,128]{1,0:T(8,128)}, f32[152,128]{1,0:T(8,128)S(1)}, u32[]{:S(2)}) copy-start(f32[152,128]{1,0:T(8,128)S(1)} %add.36.mine_ref) | copy-start | bytes 233476
  245.6 4.4 %collective-permute-start.8 = (f32[152,128]{1,0:T(8,128)S(1)}, f32[152,128]{1,0:T(8,128)S(1)}, u32[]{:S(2)}, u32[]{:S(2)}) collective-permute-start(f32[152,128]{1,0:T(8,128)S(1)} %add.36.mine_ref), channel_id=1, source_target_pairs={{0,4},{4,0},{8,12},{12,8},{16,20},{20,16},{24,28},{28,24},{32,36},... | collective-permute-start | bytes 233480 | tf_op jit(solution)/shard_map/ppermute | solution.py:286
  249.9 0.6 copy-start.14

commit v3 on v2

--- a/solution.py
+++ b/solution.py
@@ -15,8 +15,8 @@
 PARTS = 64
 ROWS = 8
 OUTER_LIMIT = 62
-CHUNKS = 4
-PITCH = 520
+CHUNKS = 8
+PITCH = 521
 TABLE = 48
 
 
@@ -120,7 +120,7 @@
 
 
 def outer_kernel(r_hbm, *refs):
-    sources, (o_hbm, s_ref, x_ref, y_ref, out_ref, wire_ref, spec_ref), refs = refs[:13], refs[13:20], refs[20:]
+    sources, (o_hbm, s_ref, x_ref, y_ref, out_ref, wire_ref, spec_ref, tfb_ref, tib_ref), refs = refs[:13], refs[13:22], refs[22:]
     targets, (in_sem, side_sem, out_sem) = refs[:13], refs[13:]
     (fo_ref, tf_ref, w_ref, hid_ref, io_ref, ti_ref, iot_ref, fot_ref, hidt_ref, wt_ref, cos_ref, tabt_ref, q_ref) = targets
     size = fo_ref.shape[0]
@@ -162,18 +162,21 @@
             sends[which * CHUNKS + c].start()
 
     def load(ref, k, scale_ref):
-        scale = jnp.broadcast_to(scale_ref[:, k : k + 1], (size, lanes))
+        scale = (tfb_ref if scale_ref is tf_ref else tib_ref)[k]
         mine = pl.ds(k, size, stride=ROWS)
         return jnp.concatenate([(scale * ref[i, mine, :]).astype(BF16) for i in range(split)], 1)
 
     def store(k, scale_ref, value):
-        scale = jnp.broadcast_to(scale_ref[:, k : k + 1], (size, lanes))
+        scale = (tfb_ref if scale_ref is tf_ref else tib_ref)[k]
         for i in range(split):
             out_ref[i, k * PITCH : k * PITCH + size] = scale * value[:, i * lanes : (i + 1) * lanes]
 
     spread(0, x_ref)
     for copy in aside[:6]:
         copy.wait()
+    for k in range(ROWS):
+        for narrow, broad in ((tf_ref, tfb_ref), (ti_ref, tib_ref)):
+            broad[k] = jnp.broadcast_to(narrow[:, k : k + 1], (size, lanes))
     coming = dot(fo_ref[...], load(x_ref, 0, tf_ref)).astype(BF16)
     for k in range(ROWS):
         spectrum = coming
@@ -375,6 +378,7 @@
         scratch_shapes=[pltpu.VMEM((channels // lanes, ROWS * size, lanes), F32)] * 2
         + [pltpu.VMEM((channels // lanes, ROWS * PITCH, lanes), F32)]
         + [pltpu.VMEM(wire, BF16), pltpu.VMEM(tokens, BF16)]
+        + [pltpu.VMEM((ROWS, size, lanes), F32)] * 2
         + [pltpu.VMEM(array.shape, array.dtype) for array in aside]
         + [pltpu.SemaphoreType.DMA((count,)) for count in (2 * CHUNKS, len(aside), 2 * CHUNKS)],
         compiler_params=pltpu.CompilerParams(vmem_limit_bytes=OUTER_LIMIT * MIB),

time: 252 us -> 251 us (level)
  no operation moved by 1% of the time
where the time goes in v3:
time: 251 us
  waiting for transfers between devices  163 us (65%)
  starting transfers between devices  39.6 us (16%)
  Pallas kernels  38.8 us (15%)
  local copies, waits for them, and re-layouts  9.11 us (4%)
    ppermute x9, waiting for transfers between devices, exchanged(): return lax.ppermute(value, axis, [(i, i ^ step) for i in range(count)])  86 us
    all_to_all x1, waiting for transfers between devices, shards(): lax.all_to_all(sent, 'seq', split_axis=0, concat_axis=0, tiled=True)  76.5 us
    ppermute x9, starting transfers between devices, exchanged(): return lax.ppermute(value, axis, [(i, i ^ step) for i in range(count)])  19.8 us
    pallas_call x1, Pallas kernels, shards(): pl.pallas_call(outer_kernel, out_shape=[jax.ShapeDtypeStruct(wire, BF16),...  14.8 us
    all_to_all x1, starting transfers between devices, shards(): lax.all_to_all(sent, 'seq', split_axis=0, concat_axis=0, tiled=True)  13.5 us
    pallas_call x1, Pallas kernels, shards(): pl.pallas_call(filter_kernel, grid_spec=pltpu.PrefetchScalarGridSpec(num_...  10.9 us
    unnamed x41, local copies, waits for them, and re-layouts  9.1 us
    all_to_all x1, starting transfers between devices, shards(): lax.all_to_all(returned, 'seq', split_axis=0, concat_axis=0, tiled=True)  6.3 us
  transfers between devices with their start and end apart: 11, of which 9 were waited for; matrix products, arithmetic and copies ran while one was open for 2% of the time, Pallas kernels for 7%

profile of v3, /device:TPU:1, one launch (start us, length us, event | category | flops | bytes accessed | tf_op | source)
XLA Modules:
  0.0 251.1 jit_solution(13093105912695290193)
XLA Ops:
  0.6 6.1 %inner_transforms.1 = bf16[64,2,64,256]{3,2,1,0:T(8,128)(2,1)} custom-call(bf16[8,512,256]{2,1,0:T(8,128)(2,1)} %bitcast.15, bf16[8,512,256]{2,1,0:T(8,128)(2,1)} %bitcast.16, bf16[8,512,256]{2,1,0:T(8,128)(2,1)} %bitcast.12, bf16[512,512]{1,0:T(8,128)(2,1)} %fi_ref.1, bf16[512,512]{1,0:T(8,128)(2,1)} %ii_ref.1), custom_call_target="tpu_custom_call" | custom-call | flops 2147483648 | bytes 10485760 | tf_op jit(solution)/shard_map/inner_transforms/pallas_call | solution.py:326
  6.7 0.0 copy-start.12
  6.7 0.0 copy-start.11
  6.8 13.5 %all-to-all-start = ((bf16[64,2,64,256]{3,2,1,0:T(8,128)(2,1)}), bf16[64,2,64,256]{3,2,1,0:T(8,128)(2,1)}, u32[]{:S(2)}, u32[]{:S(2)}) async-start(bf16[64,2,64,256]{3,2,1,0:T(8,128)(2,1)} %inner_transforms.1), calls=%async_computation | async-start | bytes 8388608 | tf_op jit(solution)/shard_map/all_to_all | solution.py:341
  20.3 0.0 copy-start.16
  20.3 0.0 copy-start.17
  20.3 0.0 copy-start.15
  20.3 0.0 copy-start.3
  20.3 0.0 copy-start.4
  20.3 0.0 copy-start.5
  20.3 1.0 copy.19
  21.3 1.0 copy.20
  22.4 0.9 copy.22.refs_1_
  23.2 0.8 copy.23.refs_5_
  24.1 0.7 copy.21
  24.8 10.9 %filter_generator.1 = (bf16[8,512,128]{2,1,0:T(8,128)(2,1)S(1)}, bf16[8,128,512]{2,1,0:T(8,128)(2,1)S(1)}, f32[8,512,128]{2,1,0:T(8,128)S(1)}, f32[8,32,128]{2,1,0:T(8,128)S(1)}) custom-call(s32[1]{0:T(128)} %bitcast.3.col_ref, f32[512,48]{1,0:T(8,128)S(1)} %copy-done.5, f32[32,128]{1,0:T(8,128)S(1)} %copy-done.3, f32[1,128]{1,0:T(1,128)S(1)} %bitcast.14), custom_call_target="tpu_custom_call" | custom-call | flops 41943040 | bytes 9437184 | tf_op jit(solution)/shard_map/filter_generator/pallas_call | solution.py:351
  35.7 0.0 copy-start.6
  35.7 1.3 copy-done.6
  37.0 1.0 copy-done.7
  38.0 1.0 copy-done.8
  39.0 0.7 copy-done.9
  39.6 76.5 %all-to-all-done.r_hbm = bf16[64,2,64,256]{3,2,1,0:T(8,128)(2,1)} async-done(((bf16[64,2,64,256]{3,2,1,0:T(8,128)(2,1)}), bf16[64,2,64,256]{3,2,1,0:T(8,128)(2,1)}, u32[]{:S(2)}, u32[]{:S(2)}) %all-to-all-start) | async-done | bytes 4194336 | tf_op jit(solution)/shard_map/all_to_all | solution.py:341
  116.1 14.8 %outer_transforms.1 = (bf16[64,2,64,256]{3,2,1,0:T(8,128)(2,1)}, f32[304,128]{1,0:T(8,128)}) custom-call(bf16[64,2,64,256]{3,2,1,0:T(8,128)(2,1)} %all-to-all-done.r_hbm, bf16[512,512]{1,0:T(8,128)(2,1)} %refs_0_.1, f32[512,8]{1,0:T(8,128)} %copy.22.refs_1_, bf16[128,256]{1,0:T(8,128)(2,1)} %refs_2_.1, bf16[8,512,128]{2,1,0:T(8,128)(2,1)} %copy-done.7, ...), custom_call_target="tpu_custom_call" | custom-call | flops 5368709120 | bytes 18874368 | tf_op jit(solution)/shard_map/outer_transforms/pallas_call | solution.py:373
  130.9 0.0 copy-start
  130.9 0.0 copy-start.1
  130.9 0.0 copy-start.2
  131.0 6.3 %all-to-all-start.1 = ((bf16[64,2,64,256]{3,2,1,0:T(8,128)(2,1)}), bf16[64,2,64,256]{3,2,1,0:T(8,128)(2,1)}, u32[]{:S(2)}, u32[]{:S(2)}) async-start(bf16[64,2,64,256]{3,2,1,0:T(8,128)(2,1)} %get-tuple-element.25), calls=%async_computation.1 | async-start | bytes 8388608 | tf_op jit(solution)/shard_map/all_to_all | solution.py:389
  137.3 1.3 collective-permute-start
  138.6 1.9 collective-permute-done
  140.5 2.8 %collective-permute-start.1 = (f32[48,128]{1,0:T(8,128)S(1)}, f32[48,128]{1,0:T(8,128)S(1)}, u32[]{:S(2)}, u32[]{:S(2)}) collective-permute-start(f32[48,128]{1,0:T(8,128)S(1)} %slice_add_fusion), channel_id=1, source_target_pairs={{0,2},{1,3},{2,0},{3,1},{4,6},{5,7},{6,4},{7,5},{8,10},{9,11},{10,... | collective-permute-start | bytes 73736 | tf_op jit(solution)/shard_map/ppermute | solution.py:289
  143.2 1.8 collective-permute-done.1
  145.1 2.1 collective-permute-start.2
  147.2 0.9 collective-permute-done.2
  148.1 1.3 collective-permute-start.3
  149.4 5.8 %collective-permute-done.3 = f32[152,128]{1,0:T(8,128)S(1)} collective-permute-done((f32[152,128]{1,0:T(8,128)S(1)}, f32[152,128]{1,0:T(8,128)S(1)}, u32[]{:S(2)}, u32[]{:S(2)}) %collective-permute-start.3) | collective-permute-done | bytes 77856 | tf_op jit(solution)/shard_map/ppermute | solution.py:289
  155.2 2.8 %collective-permute-start.4 = (f32[152,128]{1,0:T(8,128)S(1)}, f32[152,128]{1,0:T(8,128)S(1)}, u32[]{:S(2)}, u32[]{:S(2)}) collective-permute-start(f32[152,128]{1,0:T(8,128)S(1)} %add.32), channel_id=1, source_target_pairs={{0,128},{4,132},{8,136},{12,140},{16,144},{20,148},{24,152},{28,15... | collective-permute-start | bytes 233480 | tf_op jit(solution)/shard_map/ppermute | solution.py:289
  158.0 4.6 %collective-permute-done.4 = f32[152,128]{1,0:T(8,128)S(1)} collective-permute-done((f32[152,128]{1,0:T(8,128)S(1)}, f32[152,128]{1,0:T(8,128)S(1)}, u32[]{:S(2)}, u32[]{:S(2)}) %collective-permute-start.4) | collective-permute-done | bytes 77856 | tf_op jit(solution)/shard_map/ppermute | solution.py:289
  162.7 3.5 %collective-permute-start.5 = (f32[152,128]{1,0:T(8,128)S(1)}, f32[152,128]{1,0:T(8,128)S(1)}, u32[]{:S(2)}, u32[]{:S(2)}) collective-permute-start(f32[152,128]{1,0:T(8,128)S(1)} %add.33), channel_id=1, source_target_pairs={{0,32},{4,36},{8,40},{12,44},{16,48},{20,52},{24,56},{28,60},{32,0... | collective-permute-start | bytes 233480 | tf_op jit(solution)/shard_map/ppermute | solution.py:289
  166.2 68.3 %collective-permute-done.5 = f32[152,128]{1,0:T(8,128)S(1)} collective-permute-done((f32[152,128]{1,0:T(8,128)S(1)}, f32[152,128]{1,0:T(8,128)S(1)}, u32[]{:S(2)}, u32[]{:S(2)}) %collective-permute-start.5) | collective-permute-done | bytes 77856 | tf_op jit(solution)/shard_map/ppermute | solution.py:289
  234.5 0.1 collective-permute-start.6
  234.6 5.5 %token_gradients.1 = (bf16[8,512,256]{2,1,0:T(8,128)(2,1)}, bf16[8,512,256]{2,1,0:T(8,128)(2,1)}) custom-call(bf16[64,2,64,256]{3,2,1,0:T(8,128)(2,1)} %all-to-all-done.1.x_hbm, bf16[8,512,256]{2,1,0:T(8,128)(2,1)S(1)} %bitcast.13, bf16[512,512]{1,0:T(8,128)(2,1)S(1)} %copy-done.2, bf16[512,512]{1,0:T(8,128)(2,1)S(1)} %copy-done.1), custom_call_target="tpu_custom_call" | custom-call | flops 2147483648 | bytes 10485760 | tf_op jit(solution)/shard_map/token_gradients/pallas_call | solution.py:401
  240.2 0.0 collective-permute-done.6
  240.2 2.4 collective-permute-start.7
  242.6 1.8 collective-permute-done.7
  244.4 3.5 %collective-permute-start.8 = (f32[152,128]{1,0:T(8,128)S(1)}, f32[152,128]{1,0:T(8,128)S(1)}, u32[]{:S(2)}, u32[]{:S(2)}) collective-permute-start(f32[152,128]{1,0:T(8,128)S(1)} %add.36.mine_ref), channel_id=1, source_target_pairs={{0,4},{4,0},{8,12},{12,8},{16,20},{20,16},{24,28},{28,24},{32,36},... | collective-permute-start | bytes 233480 | tf_op jit(solution)/shard_map/ppermute | solution.py:289
  247.9 0.9 collective-permute-done.8.other_ref
  248.8 0.6 copy-done.14
  249.5 1.6 weight_gradients.1
  (31 shorter events, 0.2 us)
Async XLA Ops:
  6.7 13.5 %copy-start.12 = (bf16[512,512]{1,0:T(8,128)(2,1)S(1)}, bf16[512,512]{1,0:T(8,128)(2,1)}, u32[]{:S(2)}) copy-start(bf16[512,512]{1,0:T(8,128)(2,1)} %refs_4_.1) | copy-start | bytes 1572868
  6.7 14.6 %copy-start.11 = (bf16[512,512]{1,0:T(8,128)(2,1)S(1)}, bf16[512,512]{1,0:T(8,128)(2,1)}, u32[]{:S(2)}) copy-start(bf16[512,512]{1,0:T(8,128)(2,1)} %refs_0_.1) | copy-start | bytes 1572868
  6.8 109.4 %all-to-all-start = ((bf16[64,2,64,256]{3,2,1,0:T(8,128)(2,1)}), bf16[64,2,64,256]{3,2,1,0:T(8,128)(2,1)}, u32[]{:S(2)}, u32[]{:S(2)}) async-start(bf16[64,2,64,256]{3,2,1,0:T(8,128)(2,1)} %inner_transforms.1), calls=%async_computation | async-start | bytes 8388608 | tf_op jit(solution)/shard_map/all_to_all | solution.py:341
  20.3 2.1 copy-start.16
  20.3 2.9 %copy-start.17 = (f32[512,8]{0,1:T(8,128)S(1)}, f32[512,8]{0,1:T(8,128)}, u32[]{:S(2)}) copy-start(f32[512,8]{0,1:T(8,128)} %param.22) | copy-start | bytes 49156
  20.3 3.8 %copy-start.15 = (bf16[128,256]{1,0:T(8,128)(2,1)S(1)}, bf16[128,256]{1,0:T(8,128)(2,1)}, u32[]{:S(2)}) copy-start(bf16[128,256]{1,0:T(8,128)(2,1)} %refs_2_.1) | copy-start | bytes 196612
  20.3 4.5 %copy-start.3 = (f32[32,128]{1,0:T(8,128)S(1)}, f32[32,128]{1,0:T(8,128)}, u32[]{:S(2)}) copy-start(f32[32,128]{1,0:T(8,128)} %fin_ref.1) | copy-start | bytes 49156
  20.3 4.5 %copy-start.4 = (f32[128]{0:T(128)S(1)}, f32[128]{0:T(128)}, u32[]{:S(2)}) copy-start(f32[128]{0:T(128)} %param.24) | copy-start | bytes 1540
  20.3 4.5 %copy-start.5 = (f32[512,48]{1,0:T(8,128)S(1)}, f32[512,48]{1,0:T(8,128)}, u32[]{:S(2)}) copy-start(f32[512,48]{1,0:T(8,128)} %constant.27.clone.tab_ref) | copy-start | bytes 294916
  35.7 1.3 copy-start.6
  37.0 1.0 copy-start.7
  38.0 1.0 copy-start.8
  39.0 0.7 copy-start.9
  130.9 6.4 %copy-start.10 = (f32[304,128]{1,0:T(8,128)S(1)}, f32[304,128]{1,0:T(8,128)}, u32[]{:S(2)}) copy-start(f32[304,128]{1,0:T(8,128)} %get-tuple-element.28) | copy-start | bytes 466948
  130.9 103.7 %copy-start = (bf16[4096,256]{1,0:T(8,128)(2,1)S(1)}, bf16[4096,256]{1,0:T(8,128)(2,1)}, u32[]{:S(2)}) copy-start(bf16[4096,256]{1,0:T(8,128)(2,1)} %param.16) | copy-start | bytes 6291460
  130.9 103.7 %copy-start.1 = (bf16[512,512]{1,0:T(8,128)(2,1)S(1)}, bf16[512,512]{1,0:T(8,128)(2,1)}, u32[]{:S(2)}) copy-start(bf16[512,512]{1,0:T(8,128)(2,1)} %fi_ref.1) | copy-start | bytes 1572868
  130.9 103.7 %copy-start.2 = (bf16[512,512]{1,0:T(8,128)(2,1)S(1)}, bf16[512,512]{1,0:T(8,128)(2,1)}, u32[]{:S(2)}) copy-start(bf16[512,512]{1,0:T(8,128)(2,1)} %ii_ref.1) | copy-start | bytes 1572868
  131.0 103.7 %all-to-all-start.1 = ((bf16[64,2,64,256]{3,2,1,0:T(8,128)(2,1)}), bf16[64,2,64,256]{3,2,1,0:T(8,128)(2,1)}, u32[]{:S(2)}, u32[]{:S(2)}) async-start(bf16[64,2,64,256]{3,2,1,0:T(8,128)(2,1)} %get-tuple-element.25), calls=%async_computation.1 | async-start | bytes 8388608 | tf_op jit(solution)/shard_map/all_to_all | solution.py:389
  137.3 3.2 %collective-permute-start = (f32[48,128]{1,0:T(8,128)S(1)}, f32[48,128]{1,0:T(8,128)S(1)}, u32[]{:S(2)}, u32[]{:S(2)}) collective-permute-start(f32[48,128]{1,0:T(8,128)S(1)} %slice.15), channel_id=1, source_target_pairs={{0,1},{1,0},{2,3},{3,2},{4,5},{5,4},{6,7},{7,6},{8,9},{9,8},{10,11... | collective-permute-start | bytes 73736 | tf_op jit(solution)/shard_map/ppermute | solution.py:289
  140.5 4.6 %collective-permute-start.1 = (f32[48,128]{1,0:T(8,128)S(1)}, f32[48,128]{1,0:T(8,128)S(1)}, u32[]{:S(2)}, u32[]{:S(2)}) collective-permute-start(f32[48,128]{1,0:T(8,128)S(1)} %slice_add_fusion), channel_id=1, source_target_pairs={{0,2},{1,3},{2,0},{3,1},{4,6},{5,7},{6,4},{7,5},{8,10},{9,11},{10,... | collective-permute-start | bytes 73736 | tf_op jit(solution)/shard_map/ppermute | solution.py:289
  145.1 3.0 %collective-permute-start.2 = (f32[152,128]{1,0:T(8,128)S(1)}, f32[152,128]{1,0:T(8,128)S(1)}, u32[]{:S(2)}, u32[]{:S(2)}) collective-permute-start(f32[152,128]{1,0:T(8,128)S(1)} %slice_select_fusion), channel_id=1, source_target_pairs={{0,4},{4,0},{8,12},{12,8},{16,20},{20,16},{24,28},{28,24},{32,36},... | collective-permute-start | bytes 233480 | tf_op jit(solution)/shard_map/ppermute | solution.py:289
  148.1 7.1 %collective-permute-start.3 = (f32[152,128]{1,0:T(8,128)S(1)}, f32[152,128]{1,0:T(8,128)S(1)}, u32[]{:S(2)}, u32[]{:S(2)}) collective-permute-start(f32[152,128]{1,0:T(8,128)S(1)} %select_add_fusion), channel_id=1, source_target_pairs={{0,64},{4,68},{8,72},{12,76},{16,80},{20,84},{24,88},{28,92},{32,9... | collective-permute-start | bytes 233480 | tf_op jit(solution)/shard_map/ppermute | solution.py:289
  155.2 7.5 %collective-permute-start.4 = (f32[152,128]{1,0:T(8,128)S(1)}, f32[152,128]{1,0:T(8,128)S(1)}, u32[]{:S(2)}, u32[]{:S(2)}) collective-permute-start(f32[152,128]{1,0:T(8,128)S(1)} %add.32), channel_id=1, source_target_pairs={{0,128},{4,132},{8,136},{12,140},{16,144},{20,148},{24,152},{28,15... | collective-permute-start | bytes 233480 | tf_op jit(solution)/shard_map/ppermute | solution.py:289
  162.7 71.8 %collective-permute-start.5 = (f32[152,128]{1,0:T(8,128)S(1)}, f32[152,128]{1,0:T(8,128)S(1)}, u32[]{:S(2)}, u32[]{:S(2)}) collective-permute-start(f32[152,128]{1,0:T(8,128)S(1)} %add.33), channel_id=1, source_target_pairs={{0,32},{4,36},{8,40},{12,44},{16,48},{20,52},{24,56},{28,60},{32,0... | collective-permute-start | bytes 233480 | tf_op jit(solution)/shard_map/ppermute | solution.py:289
  234.5 5.7 %collective-permute-start.6 = (f32[152,128]{1,0:T(8,128)S(1)}, f32[152,128]{1,0:T(8,128)S(1)}, u32[]{:S(2)}, u32[]{:S(2)}) collective-permute-start(f32[152,128]{1,0:T(8,128)S(1)} %add.34), channel_id=1, source_target_pairs={{0,16},{4,20},{8,24},{12,28},{16,0},{20,4},{24,8},{28,12},{32,48},... | collective-permute-start | bytes 233480 | tf_op jit(solution)/shard_map/ppermute | solution.py:289
  240.2 4.2 %collective-permute-start.7 = (f32[152,128]{1,0:T(8,128)S(1)}, f32[152,128]{1,0:T(8,128)S(1)}, u32[]{:S(2)}, u32[]{:S(2)}) collective-permute-start(f32[152,128]{1,0:T(8,128)S(1)} %add.35), channel_id=1, source_target_pairs={{0,8},{4,12},{8,0},{12,4},{16,24},{20,28},{24,16},{28,20},{32,40},... | collective-permute-start | bytes 233480 | tf_op jit(solution)/shard_map/ppermute | solution.py:289
  244.4 4.4 %copy-start.13 = (f32[152,128]{1,0:T(8,128)}, f32[152,128]{1,0:T(8,128)S(1)}, u32[]{:S(2)}) copy-start(f32[152,128]{1,0:T(8,128)S(1)} %add.36.mine_ref) | copy-start | bytes 233476
  244.4 4.4 %collective-permute-start.8 = (f32[152,128]{1,0:T(8,128)S(1)}, f32[152,128]{1,0:T(8,128)S(1)}, u32[]{:S(2)}, u32[]{:S(2)}) collective-permute-start(f32[152,128]{1,0:T(8,128)S(1)} %add.36.mine_ref), channel_id=1, source_target_pairs={{0,4},{4,0},{8,12},{12,8},{16,20},{20,16},{24,28},{28,24},{32,36},... | collective-permute-start | bytes 233480 | tf_op jit(solution)/shard_map/ppermute | solution.py:289
  248.8 0.6 copy-start.14

commit v4 on v3

--- a/solution.py
+++ b/solution.py
@@ -187,7 +187,7 @@
         store(k, ti_ref, dot(io_ref[...], filtered))
     spread(1, y_ref)
     send(0)
-    for copy in aside[6:]:
+    for copy in aside[6:8]:
         copy.wait()
 
     weight = jnp.zeros((hidden, channels), F32)
@@ -195,6 +195,8 @@
     bias = jnp.zeros((TABLE - 2 * halves, hidden), F32)
     pending = []
     coming = dot(iot_ref[...], load(y_ref, 0, ti_ref))
+    for copy in aside[8:]:
+        copy.wait()
     for k in range(ROWS):
         grad_filtered = coming
         if k + 1 < ROWS:

time: 251 us -> 252 us (level)
  no operation moved by 1% of the time
where the time goes in v4:
time: 252 us; the launch traced here: 251 us
  waiting for transfers between devices  162 us (64%)
  starting transfers between devices  39.5 us (16%)
  Pallas kernels  39.3 us (16%)
  local copies, waits for them, and re-layouts  9.11 us (4%)
    ppermute x9, waiting for transfers between devices, exchanged(): return lax.ppermute(value, axis, [(i, i ^ step) for i in range(count)])  86.1 us
    all_to_all x1, waiting for transfers between devices, shards(): lax.all_to_all(sent, 'seq', split_axis=0, concat_axis=0, tiled=True)  76.3 us
    ppermute x9, starting transfers between devices, exchanged(): return lax.ppermute(value, axis, [(i, i ^ step) for i in range(count)])  19.8 us
    pallas_call x1, Pallas kernels, shards(): pl.pallas_call(outer_kernel, out_shape=[jax.ShapeDtypeStruct(wire, BF16),...  15.1 us
    all_to_all x1, starting transfers between devices, shards(): lax.all_to_all(sent, 'seq', split_axis=0, concat_axis=0, tiled=True)  13.5 us
    pallas_call x1, Pallas kernels, shards(): pl.pallas_call(filter_kernel, grid_spec=pltpu.PrefetchScalarGridSpec(num_...  11 us
    unnamed x41, local copies, waits for them, and re-layouts  9.1 us
    all_to_all x1, starting transfers between devices, shards(): lax.all_to_all(returned, 'seq', split_axis=0, concat_axis=0, tiled=True)  6.22 us
  transfers between devices with their start and end apart: 11, of which 9 were waited for; matrix products, arithmetic and copies ran while one was open for 2% of the time, Pallas kernels for 7%

profile of v4, /device:TPU:1, one launch (start us, length us, event | category | flops | bytes accessed | tf_op | source)
XLA Modules:
  0.0 251.3 jit_solution(7865703770167302050)
XLA Ops:
  0.6 6.1 %inner_transforms.1 = bf16[64,2,64,256]{3,2,1,0:T(8,128)(2,1)} custom-call(bf16[8,512,256]{2,1,0:T(8,128)(2,1)} %bitcast.15, bf16[8,512,256]{2,1,0:T(8,128)(2,1)} %bitcast.16, bf16[8,512,256]{2,1,0:T(8,128)(2,1)} %bitcast.12, bf16[512,512]{1,0:T(8,128)(2,1)} %fi_ref.1, bf16[512,512]{1,0:T(8,128)(2,1)} %ii_ref.1), custom_call_target="tpu_custom_call" | custom-call | flops 2147483648 | bytes 10485760 | tf_op jit(solution)/shard_map/inner_transforms/pallas_call | solution.py:328
  6.7 0.0 copy-start.12
  6.7 0.0 copy-start.11
  6.8 13.5 %all-to-all-start = ((bf16[64,2,64,256]{3,2,1,0:T(8,128)(2,1)}), bf16[64,2,64,256]{3,2,1,0:T(8,128)(2,1)}, u32[]{:S(2)}, u32[]{:S(2)}) async-start(bf16[64,2,64,256]{3,2,1,0:T(8,128)(2,1)} %inner_transforms.1), calls=%async_computation | async-start | bytes 8388608 | tf_op jit(solution)/shard_map/all_to_all | solution.py:343
  20.3 0.0 copy-start.16
  20.3 0.0 copy-start.17
  20.3 0.0 copy-start.15
  20.3 0.0 copy-start.3
  20.3 0.0 copy-start.4
  20.3 0.0 copy-start.5
  20.3 1.0 copy.19
  21.3 1.0 copy.20
  22.3 0.9 copy.22.refs_1_
  23.2 0.8 copy.23.refs_5_
  24.0 0.7 copy.21
  24.8 11.0 %filter_generator.1 = (bf16[8,512,128]{2,1,0:T(8,128)(2,1)S(1)}, bf16[8,128,512]{2,1,0:T(8,128)(2,1)S(1)}, f32[8,512,128]{2,1,0:T(8,128)S(1)}, f32[8,32,128]{2,1,0:T(8,128)S(1)}) custom-call(s32[1]{0:T(128)} %bitcast.3.col_ref, f32[512,48]{1,0:T(8,128)S(1)} %copy-done.5, f32[32,128]{1,0:T(8,128)S(1)} %copy-done.3, f32[1,128]{1,0:T(1,128)S(1)} %bitcast.14), custom_call_target="tpu_custom_call" | custom-call | flops 41943040 | bytes 9437184 | tf_op jit(solution)/shard_map/filter_generator/pallas_call | solution.py:353
  35.8 0.0 copy-start.6
  35.8 1.3 copy-done.6
  37.2 1.0 copy-done.7
  38.1 1.0 copy-done.8
  39.2 0.7 copy-done.9
  39.8 76.3 %all-to-all-done.r_hbm = bf16[64,2,64,256]{3,2,1,0:T(8,128)(2,1)} async-done(((bf16[64,2,64,256]{3,2,1,0:T(8,128)(2,1)}), bf16[64,2,64,256]{3,2,1,0:T(8,128)(2,1)}, u32[]{:S(2)}, u32[]{:S(2)}) %all-to-all-start) | async-done | bytes 4194336 | tf_op jit(solution)/shard_map/all_to_all | solution.py:343
  116.1 15.1 %outer_transforms.1 = (bf16[64,2,64,256]{3,2,1,0:T(8,128)(2,1)}, f32[304,128]{1,0:T(8,128)}) custom-call(bf16[64,2,64,256]{3,2,1,0:T(8,128)(2,1)} %all-to-all-done.r_hbm, bf16[512,512]{1,0:T(8,128)(2,1)} %refs_0_.1, f32[512,8]{1,0:T(8,128)} %copy.22.refs_1_, bf16[128,256]{1,0:T(8,128)(2,1)} %refs_2_.1, bf16[8,512,128]{2,1,0:T(8,128)(2,1)} %copy-done.7, ...), custom_call_target="tpu_custom_call" | custom-call | flops 5368709120 | bytes 18874368 | tf_op jit(solution)/shard_map/outer_transforms/pallas_call | solution.py:375
  131.2 0.0 copy-start
  131.3 0.0 copy-start.1
  131.3 0.0 copy-start.2
  131.3 6.2 %all-to-all-start.1 = ((bf16[64,2,64,256]{3,2,1,0:T(8,128)(2,1)}), bf16[64,2,64,256]{3,2,1,0:T(8,128)(2,1)}, u32[]{:S(2)}, u32[]{:S(2)}) async-start(bf16[64,2,64,256]{3,2,1,0:T(8,128)(2,1)} %get-tuple-element.25), calls=%async_computation.1 | async-start | bytes 8388608 | tf_op jit(solution)/shard_map/all_to_all | solution.py:391
  137.5 1.3 collective-permute-start
  138.8 1.9 collective-permute-done
  140.7 2.7 %collective-permute-start.1 = (f32[48,128]{1,0:T(8,128)S(1)}, f32[48,128]{1,0:T(8,128)S(1)}, u32[]{:S(2)}, u32[]{:S(2)}) collective-permute-start(f32[48,128]{1,0:T(8,128)S(1)} %slice_add_fusion), channel_id=1, source_target_pairs={{0,2},{1,3},{2,0},{3,1},{4,6},{5,7},{6,4},{7,5},{8,10},{9,11},{10,... | collective-permute-start | bytes 73736 | tf_op jit(solution)/shard_map/ppermute | solution.py:291
  143.5 1.8 collective-permute-done.1
  145.3 2.1 collective-permute-start.2
  147.4 0.9 collective-permute-done.2
  148.4 1.3 collective-permute-start.3
  149.7 5.8 %collective-permute-done.3 = f32[152,128]{1,0:T(8,128)S(1)} collective-permute-done((f32[152,128]{1,0:T(8,128)S(1)}, f32[152,128]{1,0:T(8,128)S(1)}, u32[]{:S(2)}, u32[]{:S(2)}) %collective-permute-start.3) | collective-permute-done | bytes 77856 | tf_op jit(solution)/shard_map/ppermute | solution.py:291
  155.5 2.8 %collective-permute-start.4 = (f32[152,128]{1,0:T(8,128)S(1)}, f32[152,128]{1,0:T(8,128)S(1)}, u32[]{:S(2)}, u32[]{:S(2)}) collective-permute-start(f32[152,128]{1,0:T(8,128)S(1)} %add.32), channel_id=1, source_target_pairs={{0,128},{4,132},{8,136},{12,140},{16,144},{20,148},{24,152},{28,15... | collective-permute-start | bytes 233480 | tf_op jit(solution)/shard_map/ppermute | solution.py:291
  158.3 4.6 %collective-permute-done.4 = f32[152,128]{1,0:T(8,128)S(1)} collective-permute-done((f32[152,128]{1,0:T(8,128)S(1)}, f32[152,128]{1,0:T(8,128)S(1)}, u32[]{:S(2)}, u32[]{:S(2)}) %collective-permute-start.4) | collective-permute-done | bytes 77856 | tf_op jit(solution)/shard_map/ppermute | solution.py:291
  162.9 3.5 %collective-permute-start.5 = (f32[152,128]{1,0:T(8,128)S(1)}, f32[152,128]{1,0:T(8,128)S(1)}, u32[]{:S(2)}, u32[]{:S(2)}) collective-permute-start(f32[152,128]{1,0:T(8,128)S(1)} %add.33), channel_id=1, source_target_pairs={{0,32},{4,36},{8,40},{12,44},{16,48},{20,52},{24,56},{28,60},{32,0... | collective-permute-start | bytes 233480 | tf_op jit(solution)/shard_map/ppermute | solution.py:291
  166.4 68.3 %collective-permute-done.5 = f32[152,128]{1,0:T(8,128)S(1)} collective-permute-done((f32[152,128]{1,0:T(8,128)S(1)}, f32[152,128]{1,0:T(8,128)S(1)}, u32[]{:S(2)}, u32[]{:S(2)}) %collective-permute-start.5) | collective-permute-done | bytes 77856 | tf_op jit(solution)/shard_map/ppermute | solution.py:291
  234.7 0.1 collective-permute-start.6
  234.9 0.0 all-to-all-done.1.x_hbm
  234.9 5.5 %token_gradients.1 = (bf16[8,512,256]{2,1,0:T(8,128)(2,1)}, bf16[8,512,256]{2,1,0:T(8,128)(2,1)}) custom-call(bf16[64,2,64,256]{3,2,1,0:T(8,128)(2,1)} %all-to-all-done.1.x_hbm, bf16[8,512,256]{2,1,0:T(8,128)(2,1)S(1)} %bitcast.13, bf16[512,512]{1,0:T(8,128)(2,1)S(1)} %copy-done.2, bf16[512,512]{1,0:T(8,128)(2,1)S(1)} %copy-done.1), custom_call_target="tpu_custom_call" | custom-call | flops 2147483648 | bytes 10485760 | tf_op jit(solution)/shard_map/token_gradients/pallas_call | solution.py:403
  240.4 2.4 collective-permute-start.7
  242.9 1.8 collective-permute-done.7
  244.7 3.5 %collective-permute-start.8 = (f32[152,128]{1,0:T(8,128)S(1)}, f32[152,128]{1,0:T(8,128)S(1)}, u32[]{:S(2)}, u32[]{:S(2)}) collective-permute-start(f32[152,128]{1,0:T(8,128)S(1)} %add.36.mine_ref), channel_id=1, source_target_pairs={{0,4},{4,0},{8,12},{12,8},{16,20},{20,16},{24,28},{28,24},{32,36},... | collective-permute-start | bytes 233480 | tf_op jit(solution)/shard_map/ppermute | solution.py:291
  248.2 0.9 collective-permute-done.8.other_ref
  249.1 0.6 copy-done.14
  249.7 1.6 weight_gradients.1
  (31 shorter events, 0.2 us)
Async XLA Ops:
  6.7 13.5 %copy-start.12 = (bf16[512,512]{1,0:T(8,128)(2,1)S(1)}, bf16[512,512]{1,0:T(8,128)(2,1)}, u32[]{:S(2)}) copy-start(bf16[512,512]{1,0:T(8,128)(2,1)} %refs_4_.1) | copy-start | bytes 1572868
  6.7 14.6 %copy-start.11 = (bf16[512,512]{1,0:T(8,128)(2,1)S(1)}, bf16[512,512]{1,0:T(8,128)(2,1)}, u32[]{:S(2)}) copy-start(bf16[512,512]{1,0:T(8,128)(2,1)} %refs_0_.1) | copy-start | bytes 1572868
  6.8 109.4 %all-to-all-start = ((bf16[64,2,64,256]{3,2,1,0:T(8,128)(2,1)}), bf16[64,2,64,256]{3,2,1,0:T(8,128)(2,1)}, u32[]{:S(2)}, u32[]{:S(2)}) async-start(bf16[64,2,64,256]{3,2,1,0:T(8,128)(2,1)} %inner_transforms.1), calls=%async_computation | async-start | bytes 8388608 | tf_op jit(solution)/shard_map/all_to_all | solution.py:343
  20.3 2.1 copy-start.16
  20.3 2.9 %copy-start.17 = (f32[512,8]{0,1:T(8,128)S(1)}, f32[512,8]{0,1:T(8,128)}, u32[]{:S(2)}) copy-start(f32[512,8]{0,1:T(8,128)} %param.22) | copy-start | bytes 49156
  20.3 3.8 %copy-start.15 = (bf16[128,256]{1,0:T(8,128)(2,1)S(1)}, bf16[128,256]{1,0:T(8,128)(2,1)}, u32[]{:S(2)}) copy-start(bf16[128,256]{1,0:T(8,128)(2,1)} %refs_2_.1) | copy-start | bytes 196612
  20.3 4.5 %copy-start.3 = (f32[32,128]{1,0:T(8,128)S(1)}, f32[32,128]{1,0:T(8,128)}, u32[]{:S(2)}) copy-start(f32[32,128]{1,0:T(8,128)} %fin_ref.1) | copy-start | bytes 49156
  20.3 4.5 %copy-start.4 = (f32[128]{0:T(128)S(1)}, f32[128]{0:T(128)}, u32[]{:S(2)}) copy-start(f32[128]{0:T(128)} %param.24) | copy-start | bytes 1540
  20.3 4.5 %copy-start.5 = (f32[512,48]{1,0:T(8,128)S(1)}, f32[512,48]{1,0:T(8,128)}, u32[]{:S(2)}) copy-start(f32[512,48]{1,0:T(8,128)} %constant.27.clone.tab_ref) | copy-start | bytes 294916
  35.8 1.3 copy-start.6
  37.2 1.0 copy-start.7
  38.1 1.0 copy-start.8
  39.2 0.7 copy-start.9
  131.2 6.3 %copy-start.10 = (f32[304,128]{1,0:T(8,128)S(1)}, f32[304,128]{1,0:T(8,128)}, u32[]{:S(2)}) copy-start(f32[304,128]{1,0:T(8,128)} %get-tuple-element.28) | copy-start | bytes 466948
  131.2 103.6 %copy-start = (bf16[4096,256]{1,0:T(8,128)(2,1)S(1)}, bf16[4096,256]{1,0:T(8,128)(2,1)}, u32[]{:S(2)}) copy-start(bf16[4096,256]{1,0:T(8,128)(2,1)} %param.16) | copy-start | bytes 6291460
  131.3 103.6 %copy-start.1 = (bf16[512,512]{1,0:T(8,128)(2,1)S(1)}, bf16[512,512]{1,0:T(8,128)(2,1)}, u32[]{:S(2)}) copy-start(bf16[512,512]{1,0:T(8,128)(2,1)} %fi_ref.1) | copy-start | bytes 1572868
  131.3 103.6 %copy-start.2 = (bf16[512,512]{1,0:T(8,128)(2,1)S(1)}, bf16[512,512]{1,0:T(8,128)(2,1)}, u32[]{:S(2)}) copy-start(bf16[512,512]{1,0:T(8,128)(2,1)} %ii_ref.1) | copy-start | bytes 1572868
  131.3 103.6 %all-to-all-start.1 = ((bf16[64,2,64,256]{3,2,1,0:T(8,128)(2,1)}), bf16[64,2,64,256]{3,2,1,0:T(8,128)(2,1)}, u32[]{:S(2)}, u32[]{:S(2)}) async-start(bf16[64,2,64,256]{3,2,1,0:T(8,128)(2,1)} %get-tuple-element.25), calls=%async_computation.1 | async-start | bytes 8388608 | tf_op jit(solution)/shard_map/all_to_all | solution.py:391
  137.5 3.2 %collective-permute-start = (f32[48,128]{1,0:T(8,128)S(1)}, f32[48,128]{1,0:T(8,128)S(1)}, u32[]{:S(2)}, u32[]{:S(2)}) collective-permute-start(f32[48,128]{1,0:T(8,128)S(1)} %slice.15), channel_id=1, source_target_pairs={{0,1},{1,0},{2,3},{3,2},{4,5},{5,4},{6,7},{7,6},{8,9},{9,8},{10,11... | collective-permute-start | bytes 73736 | tf_op jit(solution)/shard_map/ppermute | solution.py:291
  140.7 4.6 %collective-permute-start.1 = (f32[48,128]{1,0:T(8,128)S(1)}, f32[48,128]{1,0:T(8,128)S(1)}, u32[]{:S(2)}, u32[]{:S(2)}) collective-permute-start(f32[48,128]{1,0:T(8,128)S(1)} %slice_add_fusion), channel_id=1, source_target_pairs={{0,2},{1,3},{2,0},{3,1},{4,6},{5,7},{6,4},{7,5},{8,10},{9,11},{10,... | collective-permute-start | bytes 73736 | tf_op jit(solution)/shard_map/ppermute | solution.py:291
  145.3 3.0 %collective-permute-start.2 = (f32[152,128]{1,0:T(8,128)S(1)}, f32[152,128]{1,0:T(8,128)S(1)}, u32[]{:S(2)}, u32[]{:S(2)}) collective-permute-start(f32[152,128]{1,0:T(8,128)S(1)} %slice_select_fusion), channel_id=1, source_target_pairs={{0,4},{4,0},{8,12},{12,8},{16,20},{20,16},{24,28},{28,24},{32,36},... | collective-permute-start | bytes 233480 | tf_op jit(solution)/shard_map/ppermute | solution.py:291
  148.4 7.1 %collective-permute-start.3 = (f32[152,128]{1,0:T(8,128)S(1)}, f32[152,128]{1,0:T(8,128)S(1)}, u32[]{:S(2)}, u32[]{:S(2)}) collective-permute-start(f32[152,128]{1,0:T(8,128)S(1)} %select_add_fusion), channel_id=1, source_target_pairs={{0,64},{4,68},{8,72},{12,76},{16,80},{20,84},{24,88},{28,92},{32,9... | collective-permute-start | bytes 233480 | tf_op jit(solution)/shard_map/ppermute | solution.py:291
  155.5 7.5 %collective-permute-start.4 = (f32[152,128]{1,0:T(8,128)S(1)}, f32[152,128]{1,0:T(8,128)S(1)}, u32[]{:S(2)}, u32[]{:S(2)}) collective-permute-start(f32[152,128]{1,0:T(8,128)S(1)} %add.32), channel_id=1, source_target_pairs={{0,128},{4,132},{8,136},{12,140},{16,144},{20,148},{24,152},{28,15... | collective-permute-start | bytes 233480 | tf_op jit(solution)/shard_map/ppermute | solution.py:291
  162.9 71.8 %collective-permute-start.5 = (f32[152,128]{1,0:T(8,128)S(1)}, f32[152,128]{1,0:T(8,128)S(1)}, u32[]{:S(2)}, u32[]{:S(2)}) collective-permute-start(f32[152,128]{1,0:T(8,128)S(1)} %add.33), channel_id=1, source_target_pairs={{0,32},{4,36},{8,40},{12,44},{16,48},{20,52},{24,56},{28,60},{32,0... | collective-permute-start | bytes 233480 | tf_op jit(solution)/shard_map/ppermute | solution.py:291
  234.7 5.7 %collective-permute-start.6 = (f32[152,128]{1,0:T(8,128)S(1)}, f32[152,128]{1,0:T(8,128)S(1)}, u32[]{:S(2)}, u32[]{:S(2)}) collective-permute-start(f32[152,128]{1,0:T(8,128)S(1)} %add.34), channel_id=1, source_target_pairs={{0,16},{4,20},{8,24},{12,28},{16,0},{20,4},{24,8},{28,12},{32,48},... | collective-permute-start | bytes 233480 | tf_op jit(solution)/shard_map/ppermute | solution.py:291
  240.4 4.2 %collective-permute-start.7 = (f32[152,128]{1,0:T(8,128)S(1)}, f32[152,128]{1,0:T(8,128)S(1)}, u32[]{:S(2)}, u32[]{:S(2)}) collective-permute-start(f32[152,128]{1,0:T(8,128)S(1)} %add.35), channel_id=1, source_target_pairs={{0,8},{4,12},{8,0},{12,4},{16,24},{20,28},{24,16},{28,20},{32,40},... | collective-permute-start | bytes 233480 | tf_op jit(solution)/shard_map/ppermute | solution.py:291
  244.7 4.4 %copy-start.13 = (f32[152,128]{1,0:T(8,128)}, f32[152,128]{1,0:T(8,128)S(1)}, u32[]{:S(2)}) copy-start(f32[152,128]{1,0:T(8,128)S(1)} %add.36.mine_ref) | copy-start | bytes 233476
  244.7 4.4 %collective-permute-start.8 = (f32[152,128]{1,0:T(8,128)S(1)}, f32[152,128]{1,0:T(8,128)S(1)}, u32[]{:S(2)}, u32[]{:S(2)}) collective-permute-start(f32[152,128]{1,0:T(8,128)S(1)} %add.36.mine_ref), channel_id=1, source_target_pairs={{0,4},{4,0},{8,12},{12,8},{16,20},{20,16},{24,28},{28,24},{32,36},... | collective-permute-start | bytes 233480 | tf_op jit(solution)/shard_map/ppermute | solution.py:291
  249.1 0.6 copy-start.14
